TPU v7x, 32 devices: a whole 2x2x4 slice. The times are simulated.
32 devices in a mesh: groups: 2 (over y), row: 4 (over z), col: 4 (over x, core).
Axes of the slice: x: 2, y: 2, z: 4, core: 2. Of those that a mesh axis runs over, the one named last changes fastest.
Arguments:
- integrals: float32 [32, 16, 512], P('groups', ('row', 'col')), parts along dimension 0, may hold values from -6 to 6
- occupied: float32 [32, 16], P('groups'), parts along dimension 0, may hold values from -1.5 to 1.5
- virtual: float32 [32, 16], P('groups'), parts along dimension 0, may hold values from -1.5 to 1.5
- int_mask: int32 [8, 16, 8], P('groups', ('row', 'col')), parts along dimension 0, may hold values 0 or 1
- occ_mask: int32 [8, 4], P('groups'), parts along dimension 0, may hold values 0 or 1
- virt_mask: int32 [8, 4], P('groups'), parts along dimension 0, may hold values 0 or 1
Outputs:
- polarizability: float32 [1024, 512], P(('groups', 'row')), parts along dimension 0
There are 2 independent parts, one for each index of `groups`. A program takes and returns all parts, laid end to end along the dimension named above; each array names one. Nothing has to cross between parts.
All inputs are finite; a program needn't handle non-finite values. No bound on the sum of `int_mask` on one device may be relied on, other than what follows from the above.
Results may differ from a plain program's by a relative error of at most 0.0001.
Values sent between devices are 32-bit elements; how exact they have to be, the bound alone decides.
No kernel may reach another device: no remote copies, remote signals or barrier semaphores. Data moves between devices by JAX's collectives and lax.ppermute only.
A program may use at most 64 MiB of HBM per device.

v0:
```python
import jax
import jax.numpy as jnp
from jax import lax
from jax.sharding import PartitionSpec as P


def spread_two(mask, tile_rows, tile_cols):
    outer, inner = mask.shape
    wide = jnp.broadcast_to(mask[:, None, :, None], (outer, tile_rows, inner, tile_cols))
    return wide.reshape(outer * tile_rows, inner * tile_cols).astype(jnp.float32)


def spread_three(mask, tile_rows, tile_cols):
    outer, middle, inner = mask.shape
    wide = jnp.broadcast_to(mask[:, None, :, :, None], (outer, tile_rows, middle, inner, tile_cols))
    return wide.reshape(outer * tile_rows, middle, inner * tile_cols).astype(jnp.float32)


def per_device(integrals, occupied, virtual, int_mask, occ_mask, virt_mask):
    highest = lax.Precision.HIGHEST
    basis = occupied.shape[0]
    local_pairs = integrals.shape[1]
    aux_count = integrals.shape[2]
    green_tile = basis // occ_mask.shape[0]
    aux_tile = aux_count // int_mask.shape[2]
    row_count = lax.axis_size("row")
    col_count = lax.axis_size("col")
    int_full = integrals * spread_three(int_mask, green_tile, aux_tile)
    occ_full = occupied * spread_two(occ_mask, green_tile, green_tile)
    virt_full = virtual * spread_two(virt_mask, green_tile, green_tile)
    flat = int_full.reshape(basis, local_pairs * aux_count)
    contract_first = (((0,), (0,)), ((), ()))
    trans_virt = lax.dot_general(
        virt_full, flat, contract_first, precision=highest, preferred_element_type=jnp.float32
    )
    shaped_virt = trans_virt.reshape(row_count, col_count, local_pairs, local_pairs, aux_count)
    mirrored = lax.all_to_all(
        lax.all_to_all(shaped_virt, "row", split_axis=0, concat_axis=0, tiled=True),
        "col",
        split_axis=1,
        concat_axis=1,
        tiled=True,
    )
    trans_occ = lax.dot_general(
        occ_full, flat, contract_first, precision=highest, preferred_element_type=jnp.float32
    )
    shaped_occ = trans_occ.reshape(row_count, col_count, local_pairs, local_pairs, aux_count)
    pair_dims = (((0, 1, 2, 3), (0, 1, 3, 2)), ((), ()))
    whole = (
        lax.dot_general(
            shaped_occ, mirrored, pair_dims, precision=highest, preferred_element_type=jnp.float32
        )
        / basis
    )
    summed = lax.psum(whole, "col")
    result = lax.psum_scatter(summed, "row", scatter_dimension=0, tiled=True)
    return result


def solution(mesh):
    placed = (
        P("groups", ("row", "col"), None),
        P("groups", None),
        P("groups", None),
        P("groups", ("row", "col"), None),
        P("groups", None),
        P("groups", None),
    )
    return jax.shard_map(
        per_device,
        mesh=mesh,
        in_specs=placed,
        out_specs=P(("groups", "row"), None),
        check_vma=False,
    )
```

profile of v0, /device:TPU:0, one launch (start us, length us, event | category | flops | bytes accessed | tf_op | source)
XLA Modules:
  0.0 97.6 jit_solution(12697223429603223982)
XLA Ops:
  6.5 0.7 convert_element_type.34
  7.3 0.1 copy.14
  7.4 0.1 copy.15
  7.4 0.1 broadcast_in_dim.8
  7.5 0.1 convert_element_type.38
  7.6 0.1 broadcast_in_dim.7
  7.7 0.1 convert_element_type.36
  7.8 0.6 copy-done
  8.5 0.8 convolution_bitcast_fusion.1
  9.3 6.5 %all-to-all-start = ((f32[4,4,1,1,512]{4,1,3,2,0:T(4,128)}), f32[4,4,1,1,512]{4,1,3,2,0:T(4,128)S(1)}, u32[]{:S(2)}, u32[]{:S(2)}) async-start(f32[4,4,1,1,512]{4,1,3,2,0:T(4,128)} %convolution_bitcast_fusion.1), calls=%async_computation | async-start | bytes 65536 | tf_op jit(solution)/shard_map/all_to_all | solution.py:38
  15.7 0.1 copy.12
  15.8 0.1 copy.13
  15.9 0.1 broadcast_in_dim.6
  16.0 0.1 convert_element_type.33
  16.0 5.3 %all-to-all-done = f32[4,4,1,1,512]{4,1,3,2,0:T(4,128)S(1)} async-done(((f32[4,4,1,1,512]{4,1,3,2,0:T(4,128)}), f32[4,4,1,1,512]{4,1,3,2,0:T(4,128)S(1)}, u32[]{:S(2)}, u32[]{:S(2)}) %all-to-all-start) | async-done | bytes 32800 | tf_op jit(solution)/shard_map/all_to_all | solution.py:38
  21.4 0.6 copy.17
  22.0 3.3 %all-to-all-start.1 = ((f32[4,4,1,1,512]{4,0,3,2,1:T(4,128)}), f32[4,4,1,1,512]{4,0,3,2,1:T(4,128)S(1)}, u32[]{:S(2)}, u32[]{:S(2)}) async-start(f32[4,4,1,1,512]{4,0,3,2,1:T(4,128)} %copy.17), calls=%async_computation.1 | async-start | bytes 65536 | tf_op jit(solution)/shard_map/all_to_all | solution.py:37
  25.3 0.2 fusion.2
  25.5 3.7 %all-to-all-done.1 = f32[4,4,1,1,512]{4,0,3,2,1:T(4,128)S(1)} async-done(((f32[4,4,1,1,512]{4,0,3,2,1:T(4,128)}), f32[4,4,1,1,512]{4,0,3,2,1:T(4,128)S(1)}, u32[]{:S(2)}, u32[]{:S(2)}) %all-to-all-start.1) | async-done | bytes 32800 | tf_op jit(solution)/shard_map/all_to_all | solution.py:37
  29.2 2.0 %fusion = f32[512,512]{1,0:T(8,128)} fusion(f32[4,4,512]{2,1,0:T(4,128)S(1)} %fusion.2, f32[4,4,1,1,512]{4,0,3,2,1:T(4,128)S(1)} %all-to-all-done.1), kind=kOutput, calls=%fused_computation.1 | convolution fusion | flops 50593792 | bytes 1114112 | tf_op jit(solution)/shard_map/dot_general | solution.py:50
  31.2 0.0 all-reduce.2.cloned.1.call-start
  31.3 24.7 %reduce-scatter.2.cloned.1.call-done = f32[128,512]{1,0:T(8,128)} async-done(((f32[512,512]{1,0:T(8,128)}), f32[128,512]{1,0:T(8,128)}) %reduce-scatter.2.cloned.1.call-update) | async-done | bytes 262160 | tf_op jit(solution)/shard_map/reduce_scatter | solution.py:56
  56.0 33.1 %all-reduce.2.cloned.1.call-done = f32[128,512]{1,0:T(8,128)} async-done(((f32[128,512]{1,0:T(8,128)}), f32[128,512]{1,0:T(8,128)}) %all-reduce.2.cloned.1.call-update) | async-done | bytes 262160 | tf_op jit(solution)/shard_map/psum | solution.py:55
  89.1 1.7 %copy.33 = f32[128,512]{1,0:T(8,128)} copy(f32[128,512]{1,0:T(8,128)} %all-reduce.2.cloned.1.call-done) | data formatting | bytes 524288
  (17 shorter events, 0.1 us)
Async XLA Ops:
  6.5 0.7 copy-start.3
  6.5 0.8 copy-start.1
  7.7 0.8 copy-start
  9.2 6.5 %copy-start.4 = (s32[4,4]{1,0:T(4,128)S(1)}, s32[4,4]{1,0:T(4,128)}, u32[]{:S(2)}) copy-start(s32[4,4]{1,0:T(4,128)} %param.10) | copy-start | bytes 196
  9.3 6.6 %copy-start.2 = (f32[16,16]{1,0:T(8,128)S(1)}, f32[16,16]{1,0:T(8,128)}, u32[]{:S(2)}) copy-start(f32[16,16]{1,0:T(8,128)} %param.7) | copy-start | bytes 3076
  9.3 12.1 %all-to-all-start = ((f32[4,4,1,1,512]{4,1,3,2,0:T(4,128)}), f32[4,4,1,1,512]{4,1,3,2,0:T(4,128)S(1)}, u32[]{:S(2)}, u32[]{:S(2)}) async-start(f32[4,4,1,1,512]{4,1,3,2,0:T(4,128)} %convolution_bitcast_fusion.1), calls=%async_computation | async-start | bytes 65536 | tf_op jit(solution)/shard_map/all_to_all | solution.py:38
  22.0 7.2 %all-to-all-start.1 = ((f32[4,4,1,1,512]{4,0,3,2,1:T(4,128)}), f32[4,4,1,1,512]{4,0,3,2,1:T(4,128)S(1)}, u32[]{:S(2)}, u32[]{:S(2)}) async-start(f32[4,4,1,1,512]{4,0,3,2,1:T(4,128)} %copy.17), calls=%async_computation.1 | async-start | bytes 65536 | tf_op jit(solution)/shard_map/all_to_all | solution.py:37
  25.3 30.7 %reduce-scatter.2.cloned.1.call-start = ((), (), s32[]{:S(2)}) async-start(), calls=%async_computation.3 | async-start | bytes 1310720 | tf_op jit(solution)/shard_map/reduce_scatter | solution.py:56
  31.2 57.9 %all-reduce.2.cloned.1.call-start = ((), (), s32[]{:S(2)}) async-start(), calls=%async_computation.4 | async-start | bytes 524288 | tf_op jit(solution)/shard_map/psum | solution.py:55
Sparse Core Ops, SparseCore 0:
  31.3 24.6 reduce-scatter.1
  58.4 30.6 all-reduce.1
where the time goes:
time: 98 us; the launch traced here: 97.6 us
  waiting for transfers between devices  66.8 us (68%)
  between operations  13.5 us (14%)
  starting transfers between devices  9.8 us (10%)
  local copies, waits for them, and re-layouts  3.77 us (4%)
  matrix products  2.97 us (3%)
    psum x1, waiting for transfers between devices, per_device(): summed = lax.psum(whole, 'col')  33.1 us
    reduce_scatter x1, waiting for transfers between devices, per_device(): result = lax.psum_scatter(summed, 'row', scatter_dimension=0, tiled=True)  24.7 us
    all_to_all x1, starting transfers between devices, per_device(): lax.all_to_all(shaped_virt, 'row', split_axis=0, concat_axis=0, tiled=True)  6.45 us
    all_to_all x1, waiting for transfers between devices, per_device(): lax.all_to_all(shaped_virt, 'row', split_axis=0, concat_axis=0, tiled=True)  5.32 us
    all_to_all x1, waiting for transfers between devices, per_device(): lax.all_to_all(lax.all_to_all(shaped_virt, 'row', split_axis=0, concat_ax...  3.68 us
    all_to_all x1, starting transfers between devices, per_device(): lax.all_to_all(lax.all_to_all(shaped_virt, 'row', split_axis=0, concat_ax...  3.26 us
    unnamed x13, local copies, waits for them, and re-layouts  2.47 us
    dot_general x1, matrix products, per_device(): lax.dot_general(shaped_occ, mirrored, pair_dims, precision=highest, prefe...  2 us
  transfers between devices with their start and end apart: 4, of which 4 were waited for; matrix products, arithmetic and copies ran while one was open for 1% of the time, Pallas kernels for 0%

commit v1 on v0

--- a/solution.py
+++ b/solution.py
@@ -1,7 +1,13 @@
+import functools
+
 import jax
 import jax.numpy as jnp
 from jax import lax
+from jax.experimental import pallas as pl
+from jax.experimental.pallas import tpu as pltpu
 from jax.sharding import PartitionSpec as P
+
+HIGHEST = lax.Precision.HIGHEST
 
 
 def spread_two(mask, tile_rows, tile_cols):
@@ -16,8 +22,7 @@
     return wide.reshape(outer * tile_rows, middle, inner * tile_cols).astype(jnp.float32)
 
 
-def per_device(integrals, occupied, virtual, int_mask, occ_mask, virt_mask):
-    highest = lax.Precision.HIGHEST
+def by_reduction(integrals, occupied, virtual, int_mask, occ_mask, virt_mask):
     basis = occupied.shape[0]
     local_pairs = integrals.shape[1]
     aux_count = integrals.shape[2]
@@ -31,7 +36,7 @@
     flat = int_full.reshape(basis, local_pairs * aux_count)
     contract_first = (((0,), (0,)), ((), ()))
     trans_virt = lax.dot_general(
-        virt_full, flat, contract_first, precision=highest, preferred_element_type=jnp.float32
+        virt_full, flat, contract_first, precision=HIGHEST, preferred_element_type=jnp.float32
     )
     shaped_virt = trans_virt.reshape(row_count, col_count, local_pairs, local_pairs, aux_count)
     mirrored = lax.all_to_all(
@@ -42,19 +47,173 @@
         tiled=True,
     )
     trans_occ = lax.dot_general(
-        occ_full, flat, contract_first, precision=highest, preferred_element_type=jnp.float32
+        occ_full, flat, contract_first, precision=HIGHEST, preferred_element_type=jnp.float32
     )
     shaped_occ = trans_occ.reshape(row_count, col_count, local_pairs, local_pairs, aux_count)
     pair_dims = (((0, 1, 2, 3), (0, 1, 3, 2)), ((), ()))
     whole = (
         lax.dot_general(
-            shaped_occ, mirrored, pair_dims, precision=highest, preferred_element_type=jnp.float32
+            shaped_occ, mirrored, pair_dims, precision=HIGHEST, preferred_element_type=jnp.float32
         )
         / basis
     )
     summed = lax.psum(whole, "col")
-    result = lax.psum_scatter(summed, "row", scatter_dimension=0, tiled=True)
-    return result
+    return lax.psum_scatter(summed, "row", scatter_dimension=0, tiled=True)
+
+
+def iota(shape, dim):
+    return lax.broadcasted_iota(jnp.int32, shape, dim)
+
+
+def one_hot(rows, cols, row_tile, col_tile):
+    return (iota((rows, cols), 0) // row_tile == iota((rows, cols), 1) // col_tile).astype(jnp.float32)
+
+
+def repeat_rows(mask, tile):
+    rows = [jnp.broadcast_to(mask[i : i + 1], (tile, mask.shape[1])) for i in range(mask.shape[0])]
+    return jnp.concatenate(rows, 0)
+
+
+def dot(a, b, dims=((1,), (0,)), precision=HIGHEST):
+    return lax.dot_general(a, b, (dims, ((), ())), precision=precision, preferred_element_type=jnp.float32)
+
+
+def masking_kernel(integrals, mask, out):
+    basis, _, aux = integrals.shape
+    tiles = mask.shape[2]
+    narrow = repeat_rows(mask[:, 0, :].astype(jnp.float32), basis // mask.shape[0])
+    wide = dot(narrow, one_hot(tiles, aux, 1, aux // tiles))
+    out[...] = integrals[:, 0, :] * wide
+
+
+def split(x):
+    high = x.astype(jnp.bfloat16)
+    return high, (x - high.astype(jnp.float32)).astype(jnp.bfloat16)
+
+
+def mixing_kernel(order, owner, occupied, virtual, occ_mask, virt_mask, high, low):
+    basis = occupied.shape[0]
+    tile = basis // occ_mask.shape[0]
+    me, lane = owner[0], owner[1]
+    picked = jnp.zeros((basis, basis), jnp.int32)
+    column = iota((basis, basis), 1)
+    for j in range(basis):
+        lam = me ^ jnp.where(lane == 1, order[1][j], order[0][j])
+        picked = jnp.where(column == j, lam, picked)
+    pick = (iota((basis, basis), 0) == picked).astype(jnp.float32)
+    wide = one_hot(basis // tile, basis, 1, tile)
+    occ_full = occupied[...] * dot(repeat_rows(occ_mask[...].astype(jnp.float32), tile), wide)
+    virt_full = virtual[...] * dot(repeat_rows(virt_mask[...].astype(jnp.float32), tile), wide)
+    occ_cols = dot(occ_full, pick)
+    virt_rows = dot(pick, virt_full, ((0,), (1,)))
+    pairs = basis * basis
+    occ_wide = dot(occ_cols, one_hot(basis, pairs, 1, basis)) * (1.0 / basis)
+    cycle = (iota((basis, pairs), 0) == lax.rem(iota((basis, pairs), 1), basis)).astype(jnp.float32)
+    virt_wide = dot(virt_rows, cycle)
+    for j in range(basis):
+        mix = occ_wide * virt_wide[j : j + 1]
+        high[j * basis : (j + 1) * basis, :], low[j * basis : (j + 1) * basis, :] = split(mix)
+
+
+def product_kernel(count, *refs):
+    row, high, low = refs[:3]
+    blocks, out = refs[3 : 3 + count], refs[3 + count]
+    rows = out.shape[0]
+    whole = jnp.concatenate([b[...] for b in blocks], 0)
+    g_high, g_low = split(whole)
+    mixed = (
+        dot(high[...], g_high, precision=None)
+        + (dot(high[...], g_low, precision=None) + dot(low[...], g_high, precision=None))
+    )
+    m_high, m_low = split(mixed)
+    start = pl.multiple_of(row[0] * rows, 128)
+    at = 0
+    parts = []
+    for b in blocks:
+        parts.append(b[:, pl.ds(start, rows)])
+    own_high, own_low = split(jnp.concatenate(parts, 0))
+    first = ((0,), (0,))
+    out[...] = (
+        dot(own_high, m_high, first, None)
+        + (dot(own_high, m_low, first, None) + dot(own_low, m_high, first, None))
+    )
+
+
+VMEM = pl.BlockSpec(memory_space=pltpu.VMEM)
+SMEM = pl.BlockSpec(memory_space=pltpu.SMEM)
+
+
+def by_gathering(integrals, occupied, virtual, int_mask, occ_mask, virt_mask):
+    basis, _, aux = integrals.shape
+    axes = ("row", "col")
+    rows = lax.axis_size("row")
+    devices = rows * lax.axis_size("col")
+    units = devices // 2
+    me = lax.axis_index("row") * lax.axis_size("col") + lax.axis_index("col")
+    lane = me % 2
+
+    def exchange(block, odd, even):
+        return lax.ppermute(block, axes, [(i, i ^ (odd if i % 2 else even)) for i in range(devices)])
+
+    half = units // 2
+    first = half + 1
+    far = [k for k in range(half, units) if k != first]
+    steps = list(zip(far, range(1, half)))
+
+    mine = pl.pallas_call(
+        masking_kernel,
+        out_shape=jax.ShapeDtypeStruct((basis, aux), jnp.float32),
+        in_specs=[VMEM, VMEM],
+        out_specs=VMEM,
+    )(integrals, int_mask)
+    mate = exchange(mine, 1, 1)
+    got = [exchange(mine, 2 * first, 2 * first)]
+    both = jnp.concatenate([mine, mate], 0)
+    got += [exchange(both, 2 * odd, 2 * even) for odd, even in steps]
+    cut = (len(got) + 1) // 2
+    early = exchange(jnp.concatenate(got[:cut], 0), 1, 1)
+    late_given = jnp.concatenate(got[cut:], 0)
+    late = exchange(late_given, 1, 1)
+
+    order = []
+    for this in (0, 1):
+        reached = [[2 * first]]
+        for pair in steps:
+            reached.append([2 * pair[1 - this], 2 * pair[1 - this] + 1])
+        other = [[2 * first + 1]]
+        for pair in steps:
+            other.append([2 * pair[this] + 1, 2 * pair[this]])
+        order.append([0, 1] + sum(reached, []) + sum(other, []))
+
+    tied = lax.optimization_barrier((occupied, virtual, occ_mask, virt_mask, late_given))
+    pairs = basis * basis
+    mix = jax.ShapeDtypeStruct((pairs, pairs), jnp.bfloat16)
+    high, low = pl.pallas_call(
+        functools.partial(mixing_kernel, order),
+        out_shape=(mix, mix),
+        in_specs=[SMEM] + [VMEM] * 4,
+        out_specs=(VMEM, VMEM),
+    )(jnp.stack([me, lane]), *tied[:4])
+    blocks = [mine, mate] + got + [early, late]
+    return pl.pallas_call(
+        functools.partial(product_kernel, len(blocks)),
+        out_shape=jax.ShapeDtypeStruct((aux // rows, aux), jnp.float32),
+        in_specs=[SMEM] + [VMEM] * (2 + len(blocks)),
+        out_specs=VMEM,
+    )(lax.axis_index("row").reshape(1), high, low, *blocks)
+
+
+def per_device(*given):
+    integrals, occupied = given[0], given[1]
+    basis, local, aux = integrals.shape
+    rows, cols = lax.axis_size("row"), lax.axis_size("col")
+    devices = rows * cols
+    lighter = devices * integrals.size <= 2 * aux * aux
+    shaped = local == 1 and cols % 2 == 0 and devices & (devices - 1) == 0 and devices >= 8
+    tiled = basis % 8 == 0 and aux // rows % 128 == 0
+    if lighter and shaped and tiled:
+        return by_gathering(*given)
+    return by_reduction(*given)
 
 
 def solution(mesh):

time: 98 us -> 24.8 us (0.25)
  waiting for transfers between devices: 66.8 us -> 4.85 us
  between operations: 13.5 us -> 0.07 us
  Pallas kernels: 0 us -> 6.09 us
  matrix products: 2.97 us -> 0 us
  local copies, waits for them, and re-layouts: 3.77 us -> 1.29 us
    psum x1 -> x0, waiting for transfers between devices: 33.1 us -> none  [per_device(): summed = lax.psum(whole, 'col')]
    reduce_scatter x1 -> x0, waiting for transfers between devices: 24.7 us -> none  [per_device(): result = lax.psum_scatter(summed, 'row', scatter_dimension=0, tiled=True)]
    ppermute x0 -> x7, starting transfers between devices: none -> 10.7 us  [exchange(): lax.ppermute(block, axes, [(i, i ^ (odd if i % 2 else even)) for i in ran...]
    all_to_all x2 -> x0, starting transfers between devices: 9.71 us -> none  [the longest x1 6.45 us: per_device(): lax.all_to_all(shaped_virt, 'row', split_axis=0, concat_axis=0, tiled=True)]
    all_to_all x2 -> x0, waiting for transfers between devices: 9 us -> none  [the longest x1 5.32 us: per_device(): lax.all_to_all(shaped_virt, 'row', split_axis=0, concat_axis=0, tiled=True)]
    pallas_call x0 -> x3, Pallas kernels: none -> 6.09 us  [the longest x1 2.54 us: by_gathering(): pl.pallas_call(functools.partial(product_kernel, len(blocks)), out_shape=...]
    ppermute x0 -> x7, waiting for transfers between devices: none -> 4.85 us  [exchange(): lax.ppermute(block, axes, [(i, i ^ (odd if i % 2 else even)) for i in ran...]
    dot_general x3 -> x0, matrix products: 2.97 us -> none  [the longest x1 2 us: per_device(): lax.dot_general(shaped_occ, mirrored, pair_dims, precision=highest, prefe...]
  transfers between devices with their start and end apart: 4 -> 7, of which waited for: 4 -> 2; matrix products, arithmetic and copies ran while one was open for 1% -> 3% of each run, Pallas kernels for 0% -> 8%
where the time goes in v1:
time: 24.8 us; the launch traced here: 24.4 us
  starting transfers between devices  10.7 us (43%)
  Pallas kernels  6.09 us (25%)
  waiting for transfers between devices  4.85 us (20%)
  other arithmetic  1.45 us (6%)
  local copies, waits for them, and re-layouts  1.29 us (5%)
    ppermute x7, starting transfers between devices, exchange(): lax.ppermute(block, axes, [(i, i ^ (odd if i % 2 else even)) for i in ran...  10.7 us
    ppermute x7, waiting for transfers between devices, exchange(): lax.ppermute(block, axes, [(i, i ^ (odd if i % 2 else even)) for i in ran...  4.85 us
    pallas_call x1, Pallas kernels, by_gathering(): pl.pallas_call(functools.partial(product_kernel, len(blocks)), out_shape=...  2.54 us
    pallas_call x1, Pallas kernels, by_gathering(): pl.pallas_call(functools.partial(mixing_kernel, order), out_shape=(mix, m...  2.01 us
    pallas_call x1, Pallas kernels, by_gathering(): pl.pallas_call(masking_kernel, out_shape=jax.ShapeDtypeStruct((basis, aux...  1.53 us
    unnamed x17, local copies, waits for them, and re-layouts  1.29 us
    concatenate x1, other arithmetic, by_gathering(): both = jnp.concatenate([mine, mate], 0)  0.78 us
    another operation x1, other arithmetic, by_gathering(): jnp.stack([me, lane])  0.67 us
  transfers between devices with their start and end apart: 7, of which 2 were waited for; matrix products, arithmetic and copies ran while one was open for 3% of the time, Pallas kernels for 8%

profile of v1, /device:TPU:0, one launch (start us, length us, event | category | flops | bytes accessed | tf_op | source)
XLA Modules:
  0.0 24.4 jit_solution(579273496146527362)
XLA Ops:
  0.0 1.5 %shard_map.64.refs_3_ = f32[16,512]{1,0:T(8,128)} custom-call(f32[16,1,512]{2,1,0:T(1,128)} %integrals.1, s32[4,1,8]{2,1,0:T(1,128)} %mask.1), custom_call_target="tpu_custom_call" | custom-call | tf_op jit(solution)/shard_map/pallas_call | solution.py:163
  1.5 0.4 %collective-permute-start = (f32[16,512]{1,0:T(8,128)}, f32[16,512]{1,0:T(8,128)S(1)}, u32[]{:S(2)}, u32[]{:S(2)}) collective-permute-start(f32[16,512]{1,0:T(8,128)} %shard_map.64.refs_3_), channel_id=1, source_target_pairs={{0,1},{1,0},{2,3},{3,2},{4,5},{5,4},{6,7},{7,6},{8,9},{9,8},{10,11... | collective-permute-start | bytes 98312 | tf_op jit(solution)/shard_map/ppermute | solution.py:156
  2.0 1.1 %collective-permute-done.refs_4_ = f32[16,512]{1,0:T(8,128)S(1)} collective-permute-done((f32[16,512]{1,0:T(8,128)}, f32[16,512]{1,0:T(8,128)S(1)}, u32[]{:S(2)}, u32[]{:S(2)}) %collective-permute-start) | collective-permute-done | bytes 32800 | tf_op jit(solution)/shard_map/ppermute | solution.py:156
  3.1 0.8 %pad_maximum_fusion.1 = f32[32,512]{1,0:T(8,128)S(1)} fusion(f32[16,512]{1,0:T(8,128)S(1)} %collective-permute-done.refs_4_, f32[16,512]{1,0:T(8,128)} %shard_map.64.refs_3_), kind=kLoop, calls=%fused_computation.1 | loop fusion | flops 16384 | bytes 131072 | tf_op jit(solution)/shard_map/concatenate | solution.py:171
  3.8 2.9 %collective-permute-start.1 = (f32[32,512]{1,0:T(8,128)S(1)}, f32[32,512]{1,0:T(8,128)S(1)}, u32[]{:S(2)}, u32[]{:S(2)}) collective-permute-start(f32[32,512]{1,0:T(8,128)S(1)} %pad_maximum_fusion.1), channel_id=1, source_target_pairs={{0,4},{1,13},{2,6},{3,15},{4,0},{5,9},{6,2},{7,11},{8,12},{9,5},{1... | collective-permute-start | bytes 196616 | tf_op jit(solution)/shard_map/ppermute | solution.py:156
  6.8 3.5 %collective-permute-start.3 = (f32[16,512]{1,0:T(8,128)S(1)}, f32[16,512]{1,0:T(8,128)S(1)}, u32[]{:S(2)}, u32[]{:S(2)}) collective-permute-start(f32[16,512]{1,0:T(8,128)S(1)} %copy-done), channel_id=1, source_target_pairs={{0,10},{1,11},{2,8},{3,9},{4,14},{5,15},{6,12},{7,13},{8,2},{9,3},... | collective-permute-start | bytes 98312 | tf_op jit(solution)/shard_map/ppermute | solution.py:156
  10.3 0.5 %collective-permute-start.4 = (f32[32,512]{1,0:T(8,128)S(1)}, f32[32,512]{1,0:T(8,128)S(1)}, u32[]{:S(2)}, u32[]{:S(2)}) collective-permute-start(f32[32,512]{1,0:T(8,128)S(1)} %pad_maximum_fusion.1), channel_id=1, source_target_pairs={{0,2},{1,9},{2,0},{3,11},{4,6},{5,13},{6,4},{7,15},{8,10},{9,1},{1... | collective-permute-start | bytes 196616 | tf_op jit(solution)/shard_map/ppermute | solution.py:156
  10.8 1.4 %collective-permute-start.2 = (f32[32,512]{1,0:T(8,128)S(1)}, f32[32,512]{1,0:T(8,128)S(1)}, u32[]{:S(2)}, u32[]{:S(2)}) collective-permute-start(f32[32,512]{1,0:T(8,128)S(1)} %pad_maximum_fusion.1), channel_id=1, source_target_pairs={{0,6},{1,15},{2,4},{3,13},{4,2},{5,11},{6,0},{7,9},{8,14},{9,7},{1... | collective-permute-start | bytes 196616 | tf_op jit(solution)/shard_map/ppermute | solution.py:156
  12.2 0.0 collective-permute-done.1.refs_7_
  12.2 3.8 %collective-permute-done.2.refs_8_ = f32[32,512]{1,0:T(8,128)S(1)} collective-permute-done((f32[32,512]{1,0:T(8,128)S(1)}, f32[32,512]{1,0:T(8,128)S(1)}, u32[]{:S(2)}, u32[]{:S(2)}) %collective-permute-start.2) | collective-permute-done | bytes 65568 | tf_op jit(solution)/shard_map/ppermute | solution.py:156
  16.0 1.9 %collective-permute-start.6 = (f32[64,512]{1,0:T(8,128)S(1)}, f32[64,512]{1,0:T(8,128)S(1)}, u32[]{:S(2)}, u32[]{:S(2)}) collective-permute-start(f32[64,512]{1,0:T(8,128)S(1)} %constant_dynamic-update-slice_fusion), channel_id=1, source_target_pairs={{0,1},{1,0},{2,3},{3,2},{4,5},{5,4},{6,7},{7,6},{8,9},{9,8},{10,11... | collective-permute-start | bytes 393224 | tf_op jit(solution)/shard_map/ppermute | solution.py:156
  17.9 0.0 collective-permute-done.3.refs_5_
  17.9 0.0 collective-permute-done.4.refs_6_
  17.9 0.6 %copy-done.6 = f32[16,512]{1,0:T(8,128)} copy-done((f32[16,512]{1,0:T(8,128)}, f32[16,512]{1,0:T(8,128)S(1)}, u32[]{:S(2)}) %copy-start.6) | copy-done | bytes 32792
  18.5 0.0 copy-done.1
  18.5 0.0 collective-permute-start.5
  18.5 0.7 %pad_add_fusion.owner = s32[2]{0:T(128)} fusion(s32[1]{0:T(128)} %bitcast.2, s32[1]{0:T(128)} %bitcast.1), kind=kLoop, calls=%fused_computation.4 | loop fusion | flops 2 | bytes 16 | tf_op jit(solution)/shard_map/stack | solution.py:196
  19.2 2.0 %shard_map.65 = (bf16[256,256]{1,0:T(8,128)(2,1)}, bf16[256,256]{1,0:T(8,128)(2,1)}) custom-call(s32[2]{0:T(128)} %pad_add_fusion.owner, f32[16,16]{1,0:T(8,128)} %occupied, f32[16,16]{1,0:T(8,128)} %virtual, s32[4,4]{1,0:T(4,128)} %occ_mask, s32[4,4]{1,0:T(4,128)} %virt_mask), custom_call_target="tpu_custom_call" | custom-call | tf_op jit(solution)/shard_map/pallas_call | solution.py:191
  21.2 0.0 collective-permute-done.5.refs_9_
  21.2 0.0 collective-permute-done.6.refs_10_
  21.2 0.0 copy-start.4
  21.2 0.6 %copy-done.7 = f32[48,512]{1,0:T(8,128)} copy-done((f32[48,512]{1,0:T(8,128)}, f32[48,512]{1,0:T(8,128)S(1)}, u32[]{:S(2)}) %copy-start.7) | copy-done | bytes 98328
  21.8 0.1 copy-done.4
  21.9 2.5 %shard_map.66 = f32[128,512]{1,0:T(8,128)} custom-call(s32[1]{0:T(128)} %bitcast.refs_0_, bf16[256,256]{1,0:T(8,128)(2,1)} %get-tuple-element.15.refs_1_, bf16[256,256]{1,0:T(8,128)(2,1)} %get-tuple-element.16.refs_2_, f32[16,512]{1,0:T(8,128)} %shard_map.64.refs_3_, f32[16,512]{1,0:T(8,128)} %copy-done.5, f32[16,512]{1,0:T(8,128)} %copy-done.6, ...), custom_call_target="tpu_custom_call" | custom-call | tf_op jit(solution)/shard_map/pallas_call | solution.py:198
  (14 shorter events, 0.0 us)
Async XLA Ops:
  1.5 5.2 %copy-start = (f32[16,512]{1,0:T(8,128)S(1)}, f32[16,512]{1,0:T(8,128)}, u32[]{:S(2)}) copy-start(f32[16,512]{1,0:T(8,128)} %shard_map.64.refs_3_) | copy-start | bytes 98308
  1.5 1.5 %collective-permute-start = (f32[16,512]{1,0:T(8,128)}, f32[16,512]{1,0:T(8,128)S(1)}, u32[]{:S(2)}, u32[]{:S(2)}) collective-permute-start(f32[16,512]{1,0:T(8,128)} %shard_map.64.refs_3_), channel_id=1, source_target_pairs={{0,1},{1,0},{2,3},{3,2},{4,5},{5,4},{6,7},{7,6},{8,9},{9,8},{10,11... | collective-permute-start | bytes 98312 | tf_op jit(solution)/shard_map/ppermute | solution.py:156
  3.1 0.8 %copy-start.5 = (f32[16,512]{1,0:T(8,128)}, f32[16,512]{1,0:T(8,128)S(1)}, u32[]{:S(2)}) copy-start(f32[16,512]{1,0:T(8,128)S(1)} %collective-permute-done.refs_4_) | copy-start | bytes 98308
  3.8 8.4 %collective-permute-start.1 = (f32[32,512]{1,0:T(8,128)S(1)}, f32[32,512]{1,0:T(8,128)S(1)}, u32[]{:S(2)}, u32[]{:S(2)}) collective-permute-start(f32[32,512]{1,0:T(8,128)S(1)} %pad_maximum_fusion.1), channel_id=1, source_target_pairs={{0,4},{1,13},{2,6},{3,15},{4,0},{5,9},{6,2},{7,11},{8,12},{9,5},{1... | collective-permute-start | bytes 196616 | tf_op jit(solution)/shard_map/ppermute | solution.py:156
  6.8 11.1 %collective-permute-start.3 = (f32[16,512]{1,0:T(8,128)S(1)}, f32[16,512]{1,0:T(8,128)S(1)}, u32[]{:S(2)}, u32[]{:S(2)}) collective-permute-start(f32[16,512]{1,0:T(8,128)S(1)} %copy-done), channel_id=1, source_target_pairs={{0,10},{1,11},{2,8},{3,9},{4,14},{5,15},{6,12},{7,13},{8,2},{9,3},... | collective-permute-start | bytes 98312 | tf_op jit(solution)/shard_map/ppermute | solution.py:156
  10.3 7.6 %collective-permute-start.4 = (f32[32,512]{1,0:T(8,128)S(1)}, f32[32,512]{1,0:T(8,128)S(1)}, u32[]{:S(2)}, u32[]{:S(2)}) collective-permute-start(f32[32,512]{1,0:T(8,128)S(1)} %pad_maximum_fusion.1), channel_id=1, source_target_pairs={{0,2},{1,9},{2,0},{3,11},{4,6},{5,13},{6,4},{7,15},{8,10},{9,1},{1... | collective-permute-start | bytes 196616 | tf_op jit(solution)/shard_map/ppermute | solution.py:156
  10.8 5.2 %collective-permute-start.2 = (f32[32,512]{1,0:T(8,128)S(1)}, f32[32,512]{1,0:T(8,128)S(1)}, u32[]{:S(2)}, u32[]{:S(2)}) collective-permute-start(f32[32,512]{1,0:T(8,128)S(1)} %pad_maximum_fusion.1), channel_id=1, source_target_pairs={{0,6},{1,15},{2,4},{3,13},{4,2},{5,11},{6,0},{7,9},{8,14},{9,7},{1... | collective-permute-start | bytes 196616 | tf_op jit(solution)/shard_map/ppermute | solution.py:156
  12.2 3.8 %copy-start.2 = (f32[32,512]{1,0:T(8,128)}, f32[32,512]{1,0:T(8,128)S(1)}, u32[]{:S(2)}) copy-start(f32[32,512]{1,0:T(8,128)S(1)} %collective-permute-done.1.refs_7_) | copy-start | bytes 196612
  16.0 1.9 %copy-start.3 = (f32[32,512]{1,0:T(8,128)}, f32[32,512]{1,0:T(8,128)S(1)}, u32[]{:S(2)}) copy-start(f32[32,512]{1,0:T(8,128)S(1)} %collective-permute-done.2.refs_8_) | copy-start | bytes 196612
  16.0 5.2 %collective-permute-start.6 = (f32[64,512]{1,0:T(8,128)S(1)}, f32[64,512]{1,0:T(8,128)S(1)}, u32[]{:S(2)}, u32[]{:S(2)}) collective-permute-start(f32[64,512]{1,0:T(8,128)S(1)} %constant_dynamic-update-slice_fusion), channel_id=1, source_target_pairs={{0,1},{1,0},{2,3},{3,2},{4,5},{5,4},{6,7},{7,6},{8,9},{9,8},{10,11... | collective-permute-start | bytes 393224 | tf_op jit(solution)/shard_map/ppermute | solution.py:156
  17.9 0.6 %copy-start.6 = (f32[16,512]{1,0:T(8,128)}, f32[16,512]{1,0:T(8,128)S(1)}, u32[]{:S(2)}) copy-start(f32[16,512]{1,0:T(8,128)S(1)} %collective-permute-done.3.refs_5_) | copy-start | bytes 98308
  17.9 0.6 %copy-start.1 = (f32[32,512]{1,0:T(8,128)}, f32[32,512]{1,0:T(8,128)S(1)}, u32[]{:S(2)}) copy-start(f32[32,512]{1,0:T(8,128)S(1)} %collective-permute-done.4.refs_6_) | copy-start | bytes 196612
  18.5 2.7 %collective-permute-start.5 = (f32[48,512]{1,0:T(8,128)S(1)}, f32[48,512]{1,0:T(8,128)S(1)}, u32[]{:S(2)}, u32[]{:S(2)}) collective-permute-start(f32[48,512]{1,0:T(8,128)S(1)} %pad_maximum_fusion), channel_id=1, source_target_pairs={{0,1},{1,0},{2,3},{3,2},{4,5},{5,4},{6,7},{7,6},{8,9},{9,8},{10,11... | collective-permute-start | bytes 294920 | tf_op jit(solution)/shard_map/ppermute | solution.py:156
  21.2 0.6 %copy-start.7 = (f32[48,512]{1,0:T(8,128)}, f32[48,512]{1,0:T(8,128)S(1)}, u32[]{:S(2)}) copy-start(f32[48,512]{1,0:T(8,128)S(1)} %collective-permute-done.5.refs_9_) | copy-start | bytes 294916
  21.2 0.7 %copy-start.4 = (f32[64,512]{1,0:T(8,128)}, f32[64,512]{1,0:T(8,128)S(1)}, u32[]{:S(2)}) copy-start(f32[64,512]{1,0:T(8,128)S(1)} %collective-permute-done.6.refs_10_) | copy-start | bytes 393220

commit v2 on v1

--- a/solution.py
+++ b/solution.py
@@ -78,12 +78,11 @@
     return lax.dot_general(a, b, (dims, ((), ())), precision=precision, preferred_element_type=jnp.float32)
 
 
-def masking_kernel(integrals, mask, out):
-    basis, _, aux = integrals.shape
-    tiles = mask.shape[2]
-    narrow = repeat_rows(mask[:, 0, :].astype(jnp.float32), basis // mask.shape[0])
-    wide = dot(narrow, one_hot(tiles, aux, 1, aux // tiles))
-    out[...] = integrals[:, 0, :] * wide
+def masking_kernel(tiles, packed, out):
+    basis, aux = out.shape
+    mask = packed[:-basis, 0, :]
+    narrow = repeat_rows(mask[:, :tiles], basis // mask.shape[0])
+    out[...] = packed[-basis:, 0, :] * dot(narrow, one_hot(tiles, aux, 1, aux // tiles), precision=None)
 
 
 def split(x):
@@ -115,32 +114,25 @@
         high[j * basis : (j + 1) * basis, :], low[j * basis : (j + 1) * basis, :] = split(mix)
 
 
+def dot_split(a, b, dims=((1,), (0,))):
+    return dot(a[0], b[0], dims, None) + (dot(a[0], b[1], dims, None) + dot(a[1], b[0], dims, None))
+
+
 def product_kernel(count, *refs):
     row, high, low = refs[:3]
     blocks, out = refs[3 : 3 + count], refs[3 + count]
     rows = out.shape[0]
+    start = pl.multiple_of(row[0] * rows, 128)
+    own = jnp.concatenate([b[:, pl.ds(start, rows)] for b in blocks], 0)
+    mixed = dot_split(split(own), (high[...], low[...]), ((0,), (0,)))
     whole = jnp.concatenate([b[...] for b in blocks], 0)
-    g_high, g_low = split(whole)
-    mixed = (
-        dot(high[...], g_high, precision=None)
-        + (dot(high[...], g_low, precision=None) + dot(low[...], g_high, precision=None))
-    )
-    m_high, m_low = split(mixed)
-    start = pl.multiple_of(row[0] * rows, 128)
-    at = 0
-    parts = []
-    for b in blocks:
-        parts.append(b[:, pl.ds(start, rows)])
-    own_high, own_low = split(jnp.concatenate(parts, 0))
-    first = ((0,), (0,))
-    out[...] = (
-        dot(own_high, m_high, first, None)
-        + (dot(own_high, m_low, first, None) + dot(own_low, m_high, first, None))
-    )
+    out[...] = dot_split(split(mixed), split(whole))
 
 
 VMEM = pl.BlockSpec(memory_space=pltpu.VMEM)
 SMEM = pl.BlockSpec(memory_space=pltpu.SMEM)
+ANY = pl.BlockSpec(memory_space=pl.ANY)
+SMALL = pltpu.CompilerParams(vmem_limit_bytes=8 * 2**20)
 
 
 def by_gathering(integrals, occupied, virtual, int_mask, occ_mask, virt_mask):
@@ -155,37 +147,32 @@
     def exchange(block, odd, even):
         return lax.ppermute(block, axes, [(i, i ^ (odd if i % 2 else even)) for i in range(devices)])
 
-    half = units // 2
-    first = half + 1
-    far = [k for k in range(half, units) if k != first]
-    steps = list(zip(far, range(1, half)))
-
+    first = units - 1
+    steps = [(2, 1)] + [(k, k + 1) for k in range(3, first, 2)]
+    tiles = int_mask.shape[2]
+    kept = jnp.pad(int_mask, ((0, basis), (0, 0), (0, aux - tiles)))
+    wide_rows = jnp.pad(integrals, ((int_mask.shape[0], 0), (0, 0), (0, 0)))
+    packed = jnp.where(lax.broadcasted_iota(jnp.int32, wide_rows.shape, 0) < int_mask.shape[0], kept.astype(jnp.float32), wide_rows)
     mine = pl.pallas_call(
-        masking_kernel,
+        functools.partial(masking_kernel, tiles),
         out_shape=jax.ShapeDtypeStruct((basis, aux), jnp.float32),
-        in_specs=[VMEM, VMEM],
+        in_specs=[VMEM],
         out_specs=VMEM,
-    )(integrals, int_mask)
-    mate = exchange(mine, 1, 1)
+        compiler_params=SMALL,
+    )(packed)
+    both = jnp.concatenate([mine, exchange(mine, 1, 1)], 0)
     got = [exchange(mine, 2 * first, 2 * first)]
-    both = jnp.concatenate([mine, mate], 0)
     got += [exchange(both, 2 * odd, 2 * even) for odd, even in steps]
-    cut = (len(got) + 1) // 2
-    early = exchange(jnp.concatenate(got[:cut], 0), 1, 1)
-    late_given = jnp.concatenate(got[cut:], 0)
-    late = exchange(late_given, 1, 1)
-
     order = []
     for this in (0, 1):
-        reached = [[2 * first]]
+        mine_reached = [[2 * first]]
+        mates = [[2 * first + 1]]
         for pair in steps:
-            reached.append([2 * pair[1 - this], 2 * pair[1 - this] + 1])
-        other = [[2 * first + 1]]
-        for pair in steps:
-            other.append([2 * pair[this] + 1, 2 * pair[this]])
-        order.append([0, 1] + sum(reached, []) + sum(other, []))
-
-    tied = lax.optimization_barrier((occupied, virtual, occ_mask, virt_mask, late_given))
+            mine_reached.append([2 * pair[1 - this], 2 * pair[1 - this] + 1])
+            mates.append([2 * pair[this] + 1, 2 * pair[this]])
+        order.append([0, 1] + sum(mine_reached, []) + sum(mates, []))
+
+    owner, _ = lax.optimization_barrier((jnp.stack([me, lane]), both))
     pairs = basis * basis
     mix = jax.ShapeDtypeStruct((pairs, pairs), jnp.bfloat16)
     high, low = pl.pallas_call(
@@ -193,13 +180,16 @@
         out_shape=(mix, mix),
         in_specs=[SMEM] + [VMEM] * 4,
         out_specs=(VMEM, VMEM),
-    )(jnp.stack([me, lane]), *tied[:4])
-    blocks = [mine, mate] + got + [early, late]
+        compiler_params=SMALL,
+    )(owner, occupied, virtual, occ_mask, virt_mask)
+    given, high, low = lax.optimization_barrier((jnp.concatenate(got, 0), high, low))
+    blocks = [both] + got + [exchange(given, 1, 1)]
     return pl.pallas_call(
         functools.partial(product_kernel, len(blocks)),
         out_shape=jax.ShapeDtypeStruct((aux // rows, aux), jnp.float32),
         in_specs=[SMEM] + [VMEM] * (2 + len(blocks)),
         out_specs=VMEM,
+        compiler_params=SMALL,
     )(lax.axis_index("row").reshape(1), high, low, *blocks)
 
 

time: 24.8 us -> 16.6 us (0.67)
  Pallas kernels: 6.09 us -> 2.42 us
  starting transfers between devices: 10.7 us -> 7.98 us
  local copies, waits for them, and re-layouts: 1.29 us -> 0.62 us
  other arithmetic: 1.45 us -> 0.96 us
  waiting for transfers between devices: 4.85 us -> 4.37 us
    ppermute x7 -> x6, starting transfers between devices: 10.7 us -> 7.98 us  [exchange(): lax.ppermute(block, axes, [(i, i ^ (odd if i % 2 else even)) for i in ran...]
    pallas_call x1, Pallas kernels: 1.53 us -> 0.12 us  [by_gathering(): pl.pallas_call(functools.partial(masking_kernel, tiles), out_shape=jax.Sh...]
    pallas_call x1, Pallas kernels: 2.54 us -> 1.24 us  [by_gathering(): pl.pallas_call(functools.partial(product_kernel, len(blocks)), out_shape=...]
    pallas_call x1, Pallas kernels: 2.01 us -> 1.05 us  [by_gathering(): pl.pallas_call(functools.partial(mixing_kernel, order), out_shape=(mix, m...]
    select_n x0 -> x1, other arithmetic: none -> 0.85 us  [by_gathering(): jnp.where(lax.broadcasted_iota(jnp.int32, wide_rows.shape, 0) < int_mask....]
    concatenate x2, other arithmetic: 0.78 us -> 0.02 us  [the longest x1 0.02 us: by_gathering(): jnp.concatenate(got, 0)]
    unnamed x17 -> x8, local copies, waits for them, and re-layouts: 1.29 us -> 0.62 us
    another operation x1, other arithmetic: 0.67 us -> 0.07 us  [by_gathering(): owner, _ = lax.optimization_barrier((jnp.stack([me, lane]), both))]
  transfers between devices with their start and end apart: 7 -> 6, of which waited for: 2 -> 2; matrix products, arithmetic and copies ran while one was open for 3% -> 0% of each run, Pallas kernels for 8% -> 6%
where the time goes in v2:
time: 16.6 us; the launch traced here: 16.4 us
  starting transfers between devices  7.98 us (48%)
  waiting for transfers between devices  4.37 us (26%)
  Pallas kernels  2.42 us (15%)
  other arithmetic  0.96 us (6%)
  local copies, waits for them, and re-layouts  0.62 us (4%)
    ppermute x6, starting transfers between devices, exchange(): lax.ppermute(block, axes, [(i, i ^ (odd if i % 2 else even)) for i in ran...  7.98 us
    ppermute x6, waiting for transfers between devices, exchange(): lax.ppermute(block, axes, [(i, i ^ (odd if i % 2 else even)) for i in ran...  4.37 us
    pallas_call x1, Pallas kernels, by_gathering(): pl.pallas_call(functools.partial(product_kernel, len(blocks)), out_shape=...  1.24 us
    pallas_call x1, Pallas kernels, by_gathering(): pl.pallas_call(functools.partial(mixing_kernel, order), out_shape=(mix, m...  1.05 us
    select_n x1, other arithmetic, by_gathering(): jnp.where(lax.broadcasted_iota(jnp.int32, wide_rows.shape, 0) < int_mask....  0.85 us
    unnamed x8, local copies, waits for them, and re-layouts  0.62 us
  transfers between devices with their start and end apart: 6, of which 2 were waited for; matrix products, arithmetic and copies ran while one was open for 0% of the time, Pallas kernels for 6%

profile of v2, /device:TPU:0, one launch (start us, length us, event | category | flops | bytes accessed | tf_op | source)
XLA Modules:
  0.0 16.4 jit_solution(8313543650773643109)
XLA Ops:
  0.0 0.9 %broadcast_select_fusion.packed = f32[20,1,512]{2,1,0:T(1,128)S(1)} fusion(pred[20]{0:T(512)(128)(4,1)S(1)} %iota_compare_fusion, f32[16,1,512]{2,1,0:T(1,128)} %param.6, s32[4,1,8]{2,1,0:T(1,128)} %param.9), kind=kLoop, calls=%fused_computation.1 | loop fusion | flops 20480 | bytes 73876 | tf_op jit(solution)/shard_map/jit(_where)/select_n | solution.py:155
  0.9 0.1 shard_map.64
  1.0 0.5 %collective-permute-start.1 = (f32[16,512]{1,0:T(8,128)S(1)}, f32[16,512]{1,0:T(8,128)S(1)}, u32[]{:S(2)}, u32[]{:S(2)}) collective-permute-start(f32[16,512]{1,0:T(8,128)S(1)} %shard_map.64), channel_id=1, source_target_pairs={{0,1},{1,0},{2,3},{3,2},{4,5},{5,4},{6,7},{7,6},{8,9},{9,8},{10,11... | collective-permute-start | bytes 98312 | tf_op jit(solution)/shard_map/ppermute | solution.py:148
  1.4 5.6 %collective-permute-start = (f32[16,512]{1,0:T(8,128)S(1)}, f32[16,512]{1,0:T(8,128)S(1)}, u32[]{:S(2)}, u32[]{:S(2)}) collective-permute-start(f32[16,512]{1,0:T(8,128)S(1)} %shard_map.64), channel_id=1, source_target_pairs={{0,14},{1,15},{2,12},{3,13},{4,10},{5,11},{6,8},{7,9},{8,6},{9,7},... | collective-permute-start | bytes 98312 | tf_op jit(solution)/shard_map/ppermute | solution.py:148
  7.0 0.0 collective-permute-done.1
  7.0 0.0 copy-start
  7.0 0.0 copy-start.1
  7.0 0.3 %collective-permute-start.4 = (f32[32,512]{1,0:T(8,128)S(1)}, f32[32,512]{1,0:T(8,128)S(1)}, u32[]{:S(2)}, u32[]{:S(2)}) collective-permute-start(f32[32,512]{1,0:T(8,128)S(1)} %pad_maximum_fusion.1.refs_3_), channel_id=1, source_target_pairs={{0,12},{1,11},{2,14},{3,9},{4,8},{5,15},{6,10},{7,13},{8,4},{9,3},... | collective-permute-start | bytes 196616 | tf_op jit(solution)/shard_map/ppermute | solution.py:148
  7.3 0.8 %collective-permute-start.3 = (f32[32,512]{1,0:T(8,128)S(1)}, f32[32,512]{1,0:T(8,128)S(1)}, u32[]{:S(2)}, u32[]{:S(2)}) collective-permute-start(f32[32,512]{1,0:T(8,128)S(1)} %pad_maximum_fusion.1.refs_3_), channel_id=1, source_target_pairs={{0,8},{1,7},{2,10},{3,5},{4,12},{5,3},{6,14},{7,1},{8,0},{9,15},{1... | collective-permute-start | bytes 196616 | tf_op jit(solution)/shard_map/ppermute | solution.py:148
  8.1 0.7 %collective-permute-start.2 = (f32[32,512]{1,0:T(8,128)S(1)}, f32[32,512]{1,0:T(8,128)S(1)}, u32[]{:S(2)}, u32[]{:S(2)}) collective-permute-start(f32[32,512]{1,0:T(8,128)S(1)} %pad_maximum_fusion.1.refs_3_), channel_id=1, source_target_pairs={{0,2},{1,5},{2,0},{3,7},{4,6},{5,1},{6,4},{7,3},{8,10},{9,13},{10,... | collective-permute-start | bytes 196616 | tf_op jit(solution)/shard_map/ppermute | solution.py:148
  8.8 0.0 copy-start.3
  8.8 0.1 pad_add_fusion.owner
  8.9 0.0 copy-done
  8.9 0.0 copy-done.1
  8.9 0.6 %copy-done.3 = s32[4,4]{1,0:T(4,128)S(1)} copy-done((s32[4,4]{1,0:T(4,128)S(1)}, s32[4,4]{1,0:T(4,128)}, u32[]{:S(2)}) %copy-start.3) | copy-done | bytes 88
  9.5 0.0 copy-done.2
  9.5 1.1 %shard_map.65 = (bf16[256,256]{1,0:T(8,128)(2,1)S(1)}, bf16[256,256]{1,0:T(8,128)(2,1)S(1)}) custom-call(s32[2]{0:T(128)S(1)} %pad_add_fusion.owner, f32[16,16]{1,0:T(8,128)S(1)} %copy-done, f32[16,16]{1,0:T(8,128)S(1)} %copy-done.1, s32[4,4]{1,0:T(4,128)S(1)} %copy-done.2, s32[4,4]{1,0:T(4,128)S(1)} %copy-done.3), custom_call_target="tpu_custom_call" | custom-call | tf_op jit(solution)/shard_map/pallas_call | solution.py:178
  10.6 0.0 collective-permute-done.refs_4_
  10.6 3.0 %collective-permute-done.4.refs_7_ = f32[32,512]{1,0:T(8,128)S(1)} collective-permute-done((f32[32,512]{1,0:T(8,128)S(1)}, f32[32,512]{1,0:T(8,128)S(1)}, u32[]{:S(2)}, u32[]{:S(2)}) %collective-permute-start.4) | collective-permute-done | bytes 65568 | tf_op jit(solution)/shard_map/ppermute | solution.py:148
  13.6 0.0 collective-permute-done.3.refs_6_
  13.6 0.0 collective-permute-done.2.refs_5_
  13.6 0.2 %collective-permute-start.5 = (f32[112,512]{1,0:T(8,128)S(1)}, f32[112,512]{1,0:T(8,128)S(1)}, u32[]{:S(2)}, u32[]{:S(2)}) collective-permute-start(f32[112,512]{1,0:T(8,128)S(1)} %pad_maximum_fusion), channel_id=1, source_target_pairs={{0,1},{1,0},{2,3},{3,2},{4,5},{5,4},{6,7},{7,6},{8,9},{9,8},{10,11... | collective-permute-start | bytes 688136 | tf_op jit(solution)/shard_map/ppermute | solution.py:148
  13.8 1.4 %collective-permute-done.5.refs_8_ = f32[112,512]{1,0:T(8,128)S(1)} collective-permute-done((f32[112,512]{1,0:T(8,128)S(1)}, f32[112,512]{1,0:T(8,128)S(1)}, u32[]{:S(2)}, u32[]{:S(2)}) %collective-permute-start.5) | collective-permute-done | bytes 229408 | tf_op jit(solution)/shard_map/ppermute | solution.py:148
  15.1 1.2 %shard_map.66 = f32[128,512]{1,0:T(8,128)} custom-call(s32[1]{0:T(128)} %bitcast.refs_0_, bf16[256,256]{1,0:T(8,128)(2,1)S(1)} %get-tuple-element.14.refs_1_, bf16[256,256]{1,0:T(8,128)(2,1)S(1)} %get-tuple-element.15.refs_2_, f32[32,512]{1,0:T(8,128)S(1)} %pad_maximum_fusion.1.refs_3_, f32[16,512]{1,0:T(8,128)S(1)} %collective-permute-done.refs_4_, ...), custom_call_target="tpu_custom_call" | custom-call | tf_op jit(solution)/shard_map/pallas_call | solution.py:187
  (4 shorter events, 0.0 us)
Async XLA Ops:
  1.0 6.0 %collective-permute-start.1 = (f32[16,512]{1,0:T(8,128)S(1)}, f32[16,512]{1,0:T(8,128)S(1)}, u32[]{:S(2)}, u32[]{:S(2)}) collective-permute-start(f32[16,512]{1,0:T(8,128)S(1)} %shard_map.64), channel_id=1, source_target_pairs={{0,1},{1,0},{2,3},{3,2},{4,5},{5,4},{6,7},{7,6},{8,9},{9,8},{10,11... | collective-permute-start | bytes 98312 | tf_op jit(solution)/shard_map/ppermute | solution.py:148
  1.4 9.1 %collective-permute-start = (f32[16,512]{1,0:T(8,128)S(1)}, f32[16,512]{1,0:T(8,128)S(1)}, u32[]{:S(2)}, u32[]{:S(2)}) collective-permute-start(f32[16,512]{1,0:T(8,128)S(1)} %shard_map.64), channel_id=1, source_target_pairs={{0,14},{1,15},{2,12},{3,13},{4,10},{5,11},{6,8},{7,9},{8,6},{9,7},... | collective-permute-start | bytes 98312 | tf_op jit(solution)/shard_map/ppermute | solution.py:148
  7.0 1.9 %copy-start = (f32[16,16]{1,0:T(8,128)S(1)}, f32[16,16]{1,0:T(8,128)}, u32[]{:S(2)}) copy-start(f32[16,16]{1,0:T(8,128)} %occupied.1) | copy-start | bytes 3076
  7.0 1.9 %copy-start.1 = (f32[16,16]{1,0:T(8,128)S(1)}, f32[16,16]{1,0:T(8,128)}, u32[]{:S(2)}) copy-start(f32[16,16]{1,0:T(8,128)} %virtual.1) | copy-start | bytes 3076
  7.0 6.5 %collective-permute-start.4 = (f32[32,512]{1,0:T(8,128)S(1)}, f32[32,512]{1,0:T(8,128)S(1)}, u32[]{:S(2)}, u32[]{:S(2)}) collective-permute-start(f32[32,512]{1,0:T(8,128)S(1)} %pad_maximum_fusion.1.refs_3_), channel_id=1, source_target_pairs={{0,12},{1,11},{2,14},{3,9},{4,8},{5,15},{6,10},{7,13},{8,4},{9,3},... | collective-permute-start | bytes 196616 | tf_op jit(solution)/shard_map/ppermute | solution.py:148
  7.3 6.2 %collective-permute-start.3 = (f32[32,512]{1,0:T(8,128)S(1)}, f32[32,512]{1,0:T(8,128)S(1)}, u32[]{:S(2)}, u32[]{:S(2)}) collective-permute-start(f32[32,512]{1,0:T(8,128)S(1)} %pad_maximum_fusion.1.refs_3_), channel_id=1, source_target_pairs={{0,8},{1,7},{2,10},{3,5},{4,12},{5,3},{6,14},{7,1},{8,0},{9,15},{1... | collective-permute-start | bytes 196616 | tf_op jit(solution)/shard_map/ppermute | solution.py:148
  8.1 5.5 %collective-permute-start.2 = (f32[32,512]{1,0:T(8,128)S(1)}, f32[32,512]{1,0:T(8,128)S(1)}, u32[]{:S(2)}, u32[]{:S(2)}) collective-permute-start(f32[32,512]{1,0:T(8,128)S(1)} %pad_maximum_fusion.1.refs_3_), channel_id=1, source_target_pairs={{0,2},{1,5},{2,0},{3,7},{4,6},{5,1},{6,4},{7,3},{8,10},{9,13},{10,... | collective-permute-start | bytes 196616 | tf_op jit(solution)/shard_map/ppermute | solution.py:148
  8.8 0.7 %copy-start.3 = (s32[4,4]{1,0:T(4,128)S(1)}, s32[4,4]{1,0:T(4,128)}, u32[]{:S(2)}) copy-start(s32[4,4]{1,0:T(4,128)} %virt_mask.1) | copy-start | bytes 196
  8.8 0.7 %copy-start.2 = (s32[4,4]{1,0:T(4,128)S(1)}, s32[4,4]{1,0:T(4,128)}, u32[]{:S(2)}) copy-start(s32[4,4]{1,0:T(4,128)} %occ_mask.1) | copy-start | bytes 196
  13.6 1.6 %collective-permute-start.5 = (f32[112,512]{1,0:T(8,128)S(1)}, f32[112,512]{1,0:T(8,128)S(1)}, u32[]{:S(2)}, u32[]{:S(2)}) collective-permute-start(f32[112,512]{1,0:T(8,128)S(1)} %pad_maximum_fusion), channel_id=1, source_target_pairs={{0,1},{1,0},{2,3},{3,2},{4,5},{5,4},{6,7},{7,6},{8,9},{9,8},{10,11... | collective-permute-start | bytes 688136 | tf_op jit(solution)/shard_map/ppermute | solution.py:148

commit v3 on v2

--- a/solution.py
+++ b/solution.py
@@ -147,8 +147,9 @@
     def exchange(block, odd, even):
         return lax.ppermute(block, axes, [(i, i ^ (odd if i % 2 else even)) for i in range(devices)])
 
-    first = units - 1
-    steps = [(2, 1)] + [(k, k + 1) for k in range(3, first, 2)]
+    first = units // 2
+    far = sorted(range(first + 1, units), key=lambda k: k % 2)
+    steps = list(zip(far, range(1, first)))
     tiles = int_mask.shape[2]
     kept = jnp.pad(int_mask, ((0, basis), (0, 0), (0, aux - tiles)))
     wide_rows = jnp.pad(integrals, ((int_mask.shape[0], 0), (0, 0), (0, 0)))
@@ -182,8 +183,10 @@
         out_specs=(VMEM, VMEM),
         compiler_params=SMALL,
     )(owner, occupied, virtual, occ_mask, virt_mask)
-    given, high, low = lax.optimization_barrier((jnp.concatenate(got, 0), high, low))
-    blocks = [both] + got + [exchange(given, 1, 1)]
+    cut = len(got) // 2
+    early = exchange(jnp.concatenate(got[:cut], 0), 1, 1)
+    given, high, low = lax.optimization_barrier((jnp.concatenate(got[cut:], 0), high, low))
+    blocks = [both] + got + [early, exchange(given, 1, 1)]
     return pl.pallas_call(
         functools.partial(product_kernel, len(blocks)),
         out_shape=jax.ShapeDtypeStruct((aux // rows, aux), jnp.float32),

time: 16.6 us -> 16.2 us (0.976)
  starting transfers between devices: 7.98 us -> 8.68 us
  local copies, waits for them, and re-layouts: 0.62 us -> 0.09 us
  waiting for transfers between devices: 4.37 us -> 3.86 us
    ppermute x6 -> x7, starting transfers between devices: 7.98 us -> 8.68 us  [exchange(): lax.ppermute(block, axes, [(i, i ^ (odd if i % 2 else even)) for i in ran...]
    unnamed x8, local copies, waits for them, and re-layouts: 0.62 us -> 0.09 us
    ppermute x6 -> x7, waiting for transfers between devices: 4.37 us -> 3.86 us  [exchange(): lax.ppermute(block, axes, [(i, i ^ (odd if i % 2 else even)) for i in ran...]
  transfers between devices with their start and end apart: 6 -> 7, of which waited for: 2 -> 3; matrix products, arithmetic and copies ran while one was open for 0% -> 1% of each run, Pallas kernels for 6% -> 7%
where the time goes in v3:
time: 16.2 us; the launch traced here: 16 us
  starting transfers between devices  8.68 us (54%)
  waiting for transfers between devices  3.86 us (24%)
  Pallas kernels  2.42 us (15%)
  other arithmetic  0.96 us (6%)
    ppermute x7, starting transfers between devices, exchange(): lax.ppermute(block, axes, [(i, i ^ (odd if i % 2 else even)) for i in ran...  8.68 us
    ppermute x7, waiting for transfers between devices, exchange(): lax.ppermute(block, axes, [(i, i ^ (odd if i % 2 else even)) for i in ran...  3.86 us
    pallas_call x1, Pallas kernels, by_gathering(): pl.pallas_call(functools.partial(product_kernel, len(blocks)), out_shape=...  1.25 us
    pallas_call x1, Pallas kernels, by_gathering(): pl.pallas_call(functools.partial(mixing_kernel, order), out_shape=(mix, m...  1.05 us
    select_n x1, other arithmetic, by_gathering(): jnp.where(lax.broadcasted_iota(jnp.int32, wide_rows.shape, 0) < int_mask....  0.85 us
  transfers between devices with their start and end apart: 7, of which 3 were waited for; matrix products, arithmetic and copies ran while one was open for 1% of the time, Pallas kernels for 7%

profile of v3, /device:TPU:0, one launch (start us, length us, event | category | flops | bytes accessed | tf_op | source)
XLA Modules:
  0.0 16.0 jit_solution(16205112554547999545)
XLA Ops:
  0.0 0.9 %broadcast_select_fusion.packed = f32[20,1,512]{2,1,0:T(1,128)S(1)} fusion(pred[20]{0:T(512)(128)(4,1)S(1)} %iota_compare_fusion, f32[16,1,512]{2,1,0:T(1,128)} %param.6, s32[4,1,8]{2,1,0:T(1,128)} %param.9), kind=kLoop, calls=%fused_computation.2 | loop fusion | flops 20480 | bytes 73876 | tf_op jit(solution)/shard_map/jit(_where)/select_n | solution.py:156
  0.9 0.1 shard_map.64
  1.0 0.5 %collective-permute-start = (f32[16,512]{1,0:T(8,128)S(1)}, f32[16,512]{1,0:T(8,128)S(1)}, u32[]{:S(2)}, u32[]{:S(2)}) collective-permute-start(f32[16,512]{1,0:T(8,128)S(1)} %shard_map.64), channel_id=1, source_target_pairs={{0,1},{1,0},{2,3},{3,2},{4,5},{5,4},{6,7},{7,6},{8,9},{9,8},{10,11... | collective-permute-start | bytes 98312 | tf_op jit(solution)/shard_map/ppermute | solution.py:148
  1.4 3.6 %collective-permute-start.3 = (f32[16,512]{1,0:T(8,128)S(1)}, f32[16,512]{1,0:T(8,128)S(1)}, u32[]{:S(2)}, u32[]{:S(2)}) collective-permute-start(f32[16,512]{1,0:T(8,128)S(1)} %shard_map.64), channel_id=1, source_target_pairs={{0,8},{1,9},{2,10},{3,11},{4,12},{5,13},{6,14},{7,15},{8,0},{9,1},... | collective-permute-start | bytes 98312 | tf_op jit(solution)/shard_map/ppermute | solution.py:148
  5.1 0.0 collective-permute-done
  5.1 0.0 copy-start
  5.1 2.6 %collective-permute-start.2 = (f32[32,512]{1,0:T(8,128)S(1)}, f32[32,512]{1,0:T(8,128)S(1)}, u32[]{:S(2)}, u32[]{:S(2)}) collective-permute-start(f32[32,512]{1,0:T(8,128)S(1)} %pad_maximum_fusion.2.refs_3_), channel_id=1, source_target_pairs={{0,6},{1,15},{2,4},{3,13},{4,2},{5,11},{6,0},{7,9},{8,14},{9,7},{1... | collective-permute-start | bytes 196616 | tf_op jit(solution)/shard_map/ppermute | solution.py:148
  7.7 0.4 %collective-permute-start.1 = (f32[32,512]{1,0:T(8,128)S(1)}, f32[32,512]{1,0:T(8,128)S(1)}, u32[]{:S(2)}, u32[]{:S(2)}) collective-permute-start(f32[32,512]{1,0:T(8,128)S(1)} %pad_maximum_fusion.2.refs_3_), channel_id=1, source_target_pairs={{0,4},{1,11},{2,6},{3,9},{4,0},{5,15},{6,2},{7,13},{8,12},{9,3},{1... | collective-permute-start | bytes 196616 | tf_op jit(solution)/shard_map/ppermute | solution.py:148
  8.1 0.1 pad_add_fusion.owner
  8.2 0.5 %collective-permute-start.4 = (f32[32,512]{1,0:T(8,128)S(1)}, f32[32,512]{1,0:T(8,128)S(1)}, u32[]{:S(2)}, u32[]{:S(2)}) collective-permute-start(f32[32,512]{1,0:T(8,128)S(1)} %pad_maximum_fusion.2.refs_3_), channel_id=1, source_target_pairs={{0,2},{1,13},{2,0},{3,15},{4,6},{5,9},{6,4},{7,11},{8,10},{9,5},{1... | collective-permute-start | bytes 196616 | tf_op jit(solution)/shard_map/ppermute | solution.py:148
  8.7 0.0 copy-done
  8.7 0.0 copy-done.1
  8.7 0.1 copy-done.3
  8.8 0.0 copy-done.2
  8.8 1.1 %shard_map.65 = (bf16[256,256]{1,0:T(8,128)(2,1)S(1)}, bf16[256,256]{1,0:T(8,128)(2,1)S(1)}) custom-call(s32[2]{0:T(128)S(1)} %pad_add_fusion.owner, f32[16,16]{1,0:T(8,128)S(1)} %copy-done, f32[16,16]{1,0:T(8,128)S(1)} %copy-done.1, s32[4,4]{1,0:T(4,128)S(1)} %copy-done.2, s32[4,4]{1,0:T(4,128)S(1)} %copy-done.3), custom_call_target="tpu_custom_call" | custom-call | tf_op jit(solution)/shard_map/pallas_call | solution.py:179
  9.9 0.5 %collective-permute-done.2.refs_7_ = f32[32,512]{1,0:T(8,128)S(1)} collective-permute-done((f32[32,512]{1,0:T(8,128)S(1)}, f32[32,512]{1,0:T(8,128)S(1)}, u32[]{:S(2)}, u32[]{:S(2)}) %collective-permute-start.2) | collective-permute-done | bytes 65568 | tf_op jit(solution)/shard_map/ppermute | solution.py:148
  10.3 2.4 %collective-permute-done.1.refs_6_ = f32[32,512]{1,0:T(8,128)S(1)} collective-permute-done((f32[32,512]{1,0:T(8,128)S(1)}, f32[32,512]{1,0:T(8,128)S(1)}, u32[]{:S(2)}, u32[]{:S(2)}) %collective-permute-start.1) | collective-permute-done | bytes 65568 | tf_op jit(solution)/shard_map/ppermute | solution.py:148
  12.8 0.5 %collective-permute-start.6 = (f32[64,512]{1,0:T(8,128)S(1)}, f32[64,512]{1,0:T(8,128)S(1)}, u32[]{:S(2)}, u32[]{:S(2)}) collective-permute-start(f32[64,512]{1,0:T(8,128)S(1)} %pad_maximum_fusion), channel_id=1, source_target_pairs={{0,1},{1,0},{2,3},{3,2},{4,5},{5,4},{6,7},{7,6},{8,9},{9,8},{10,11... | collective-permute-start | bytes 393224 | tf_op jit(solution)/shard_map/ppermute | solution.py:148
  13.3 0.0 collective-permute-done.3.refs_4_
  13.3 0.0 collective-permute-done.4.refs_5_
  13.3 0.6 %collective-permute-start.5 = (f32[48,512]{1,0:T(8,128)S(1)}, f32[48,512]{1,0:T(8,128)S(1)}, u32[]{:S(2)}, u32[]{:S(2)}) collective-permute-start(f32[48,512]{1,0:T(8,128)S(1)} %pad_maximum_fusion.1), channel_id=1, source_target_pairs={{0,1},{1,0},{2,3},{3,2},{4,5},{5,4},{6,7},{7,6},{8,9},{9,8},{10,11... | collective-permute-start | bytes 294920 | tf_op jit(solution)/shard_map/ppermute | solution.py:148
  13.8 0.9 %collective-permute-done.5.refs_8_ = f32[48,512]{1,0:T(8,128)S(1)} collective-permute-done((f32[48,512]{1,0:T(8,128)S(1)}, f32[48,512]{1,0:T(8,128)S(1)}, u32[]{:S(2)}, u32[]{:S(2)}) %collective-permute-start.5) | collective-permute-done | bytes 98336 | tf_op jit(solution)/shard_map/ppermute | solution.py:148
  14.8 0.0 collective-permute-done.6.refs_9_
  14.8 1.2 %shard_map.66 = f32[128,512]{1,0:T(8,128)} custom-call(s32[1]{0:T(128)} %bitcast.refs_0_, bf16[256,256]{1,0:T(8,128)(2,1)S(1)} %get-tuple-element.14.refs_1_, bf16[256,256]{1,0:T(8,128)(2,1)S(1)} %get-tuple-element.15.refs_2_, f32[32,512]{1,0:T(8,128)S(1)} %pad_maximum_fusion.2.refs_3_, f32[16,512]{1,0:T(8,128)S(1)} %collective-permute-done.3.refs_4_, ...), custom_call_target="tpu_custom_call" | custom-call | tf_op jit(solution)/shard_map/pallas_call | solution.py:190
  (7 shorter events, 0.0 us)
Async XLA Ops:
  1.0 4.1 %collective-permute-start = (f32[16,512]{1,0:T(8,128)S(1)}, f32[16,512]{1,0:T(8,128)S(1)}, u32[]{:S(2)}, u32[]{:S(2)}) collective-permute-start(f32[16,512]{1,0:T(8,128)S(1)} %shard_map.64), channel_id=1, source_target_pairs={{0,1},{1,0},{2,3},{3,2},{4,5},{5,4},{6,7},{7,6},{8,9},{9,8},{10,11... | collective-permute-start | bytes 98312 | tf_op jit(solution)/shard_map/ppermute | solution.py:148
  1.4 11.8 %collective-permute-start.3 = (f32[16,512]{1,0:T(8,128)S(1)}, f32[16,512]{1,0:T(8,128)S(1)}, u32[]{:S(2)}, u32[]{:S(2)}) collective-permute-start(f32[16,512]{1,0:T(8,128)S(1)} %shard_map.64), channel_id=1, source_target_pairs={{0,8},{1,9},{2,10},{3,11},{4,12},{5,13},{6,14},{7,15},{8,0},{9,1},... | collective-permute-start | bytes 98312 | tf_op jit(solution)/shard_map/ppermute | solution.py:148
  5.1 3.7 %copy-start = (f32[16,16]{1,0:T(8,128)S(1)}, f32[16,16]{1,0:T(8,128)}, u32[]{:S(2)}) copy-start(f32[16,16]{1,0:T(8,128)} %occupied.1) | copy-start | bytes 3076
  5.1 3.7 %copy-start.1 = (f32[16,16]{1,0:T(8,128)S(1)}, f32[16,16]{1,0:T(8,128)}, u32[]{:S(2)}) copy-start(f32[16,16]{1,0:T(8,128)} %virtual.1) | copy-start | bytes 3076
  5.1 5.2 %collective-permute-start.2 = (f32[32,512]{1,0:T(8,128)S(1)}, f32[32,512]{1,0:T(8,128)S(1)}, u32[]{:S(2)}, u32[]{:S(2)}) collective-permute-start(f32[32,512]{1,0:T(8,128)S(1)} %pad_maximum_fusion.2.refs_3_), channel_id=1, source_target_pairs={{0,6},{1,15},{2,4},{3,13},{4,2},{5,11},{6,0},{7,9},{8,14},{9,7},{1... | collective-permute-start | bytes 196616 | tf_op jit(solution)/shard_map/ppermute | solution.py:148
  7.7 5.1 %collective-permute-start.1 = (f32[32,512]{1,0:T(8,128)S(1)}, f32[32,512]{1,0:T(8,128)S(1)}, u32[]{:S(2)}, u32[]{:S(2)}) collective-permute-start(f32[32,512]{1,0:T(8,128)S(1)} %pad_maximum_fusion.2.refs_3_), channel_id=1, source_target_pairs={{0,4},{1,11},{2,6},{3,9},{4,0},{5,15},{6,2},{7,13},{8,12},{9,3},{1... | collective-permute-start | bytes 196616 | tf_op jit(solution)/shard_map/ppermute | solution.py:148
  8.1 0.7 %copy-start.3 = (s32[4,4]{1,0:T(4,128)S(1)}, s32[4,4]{1,0:T(4,128)}, u32[]{:S(2)}) copy-start(s32[4,4]{1,0:T(4,128)} %virt_mask.1) | copy-start | bytes 196
  8.1 0.7 %copy-start.2 = (s32[4,4]{1,0:T(4,128)S(1)}, s32[4,4]{1,0:T(4,128)}, u32[]{:S(2)}) copy-start(s32[4,4]{1,0:T(4,128)} %occ_mask.1) | copy-start | bytes 196
  8.2 5.1 %collective-permute-start.4 = (f32[32,512]{1,0:T(8,128)S(1)}, f32[32,512]{1,0:T(8,128)S(1)}, u32[]{:S(2)}, u32[]{:S(2)}) collective-permute-start(f32[32,512]{1,0:T(8,128)S(1)} %pad_maximum_fusion.2.refs_3_), channel_id=1, source_target_pairs={{0,2},{1,13},{2,0},{3,15},{4,6},{5,9},{6,4},{7,11},{8,10},{9,5},{1... | collective-permute-start | bytes 196616 | tf_op jit(solution)/shard_map/ppermute | solution.py:148
  12.8 2.0 %collective-permute-start.6 = (f32[64,512]{1,0:T(8,128)S(1)}, f32[64,512]{1,0:T(8,128)S(1)}, u32[]{:S(2)}, u32[]{:S(2)}) collective-permute-start(f32[64,512]{1,0:T(8,128)S(1)} %pad_maximum_fusion), channel_id=1, source_target_pairs={{0,1},{1,0},{2,3},{3,2},{4,5},{5,4},{6,7},{7,6},{8,9},{9,8},{10,11... | collective-permute-start | bytes 393224 | tf_op jit(solution)/shard_map/ppermute | solution.py:148
  13.3 1.5 %collective-permute-start.5 = (f32[48,512]{1,0:T(8,128)S(1)}, f32[48,512]{1,0:T(8,128)S(1)}, u32[]{:S(2)}, u32[]{:S(2)}) collective-permute-start(f32[48,512]{1,0:T(8,128)S(1)} %pad_maximum_fusion.1), channel_id=1, source_target_pairs={{0,1},{1,0},{2,3},{3,2},{4,5},{5,4},{6,7},{7,6},{8,9},{9,8},{10,11... | collective-permute-start | bytes 294920 | tf_op jit(solution)/shard_map/ppermute | solution.py:148

commit v4 on v3

--- a/solution.py
+++ b/solution.py
@@ -115,7 +115,10 @@
 
 
 def dot_split(a, b, dims=((1,), (0,))):
-    return dot(a[0], b[0], dims, None) + (dot(a[0], b[1], dims, None) + dot(a[1], b[0], dims, None))
+    kept = 1 - dims[0][0]
+    count = a[0].shape[kept]
+    tall = dot(jnp.concatenate(a, kept), b[0], dims, None)
+    return tall[:count] + (tall[count:] + dot(a[0], b[1], dims, None))
 
 
 def product_kernel(count, *refs):
@@ -131,7 +134,6 @@
 
 VMEM = pl.BlockSpec(memory_space=pltpu.VMEM)
 SMEM = pl.BlockSpec(memory_space=pltpu.SMEM)
-ANY = pl.BlockSpec(memory_space=pl.ANY)
 SMALL = pltpu.CompilerParams(vmem_limit_bytes=8 * 2**20)
 
 
@@ -203,7 +205,7 @@
     devices = rows * cols
     lighter = devices * integrals.size <= 2 * aux * aux
     shaped = local == 1 and cols % 2 == 0 and devices & (devices - 1) == 0 and devices >= 8
-    tiled = basis % 8 == 0 and aux // rows % 128 == 0
+    tiled = basis % 16 == 0 and aux // rows % 128 == 0
     if lighter and shaped and tiled:
         return by_gathering(*given)
     return by_reduction(*given)

time: 16.2 us -> 16.2 us (level)
  no operation moved by 1% of the time
where the time goes in v4:
time: 16.2 us; the launch traced here: 16 us
  starting transfers between devices  8.68 us (54%)
  waiting for transfers between devices  3.86 us (24%)
  Pallas kernels  2.4 us (15%)
  other arithmetic  0.96 us (6%)
    ppermute x7, starting transfers between devices, exchange(): lax.ppermute(block, axes, [(i, i ^ (odd if i % 2 else even)) for i in ran...  8.68 us
    ppermute x7, waiting for transfers between devices, exchange(): lax.ppermute(block, axes, [(i, i ^ (odd if i % 2 else even)) for i in ran...  3.86 us
    pallas_call x1, Pallas kernels, by_gathering(): pl.pallas_call(functools.partial(product_kernel, len(blocks)), out_shape=...  1.22 us
    pallas_call x1, Pallas kernels, by_gathering(): pl.pallas_call(functools.partial(mixing_kernel, order), out_shape=(mix, m...  1.05 us
    select_n x1, other arithmetic, by_gathering(): jnp.where(lax.broadcasted_iota(jnp.int32, wide_rows.shape, 0) < int_mask....  0.85 us
  transfers between devices with their start and end apart: 7, of which 3 were waited for; matrix products, arithmetic and copies ran while one was open for 1% of the time, Pallas kernels for 7%

profile of v4, /device:TPU:0, one launch (start us, length us, event | category | flops | bytes accessed | tf_op | source)
XLA Modules:
  0.0 16.0 jit_solution(16192941885356081273)
XLA Ops:
  0.0 0.9 %broadcast_select_fusion.packed = f32[20,1,512]{2,1,0:T(1,128)S(1)} fusion(pred[20]{0:T(512)(128)(4,1)S(1)} %iota_compare_fusion, f32[16,1,512]{2,1,0:T(1,128)} %param.6, s32[4,1,8]{2,1,0:T(1,128)} %param.9), kind=kLoop, calls=%fused_computation.2 | loop fusion | flops 20480 | bytes 73876 | tf_op jit(solution)/shard_map/jit(_where)/select_n | solution.py:158
  0.9 0.1 shard_map.64
  1.0 0.5 %collective-permute-start = (f32[16,512]{1,0:T(8,128)S(1)}, f32[16,512]{1,0:T(8,128)S(1)}, u32[]{:S(2)}, u32[]{:S(2)}) collective-permute-start(f32[16,512]{1,0:T(8,128)S(1)} %shard_map.64), channel_id=1, source_target_pairs={{0,1},{1,0},{2,3},{3,2},{4,5},{5,4},{6,7},{7,6},{8,9},{9,8},{10,11... | collective-permute-start | bytes 98312 | tf_op jit(solution)/shard_map/ppermute | solution.py:150
  1.4 3.6 %collective-permute-start.3 = (f32[16,512]{1,0:T(8,128)S(1)}, f32[16,512]{1,0:T(8,128)S(1)}, u32[]{:S(2)}, u32[]{:S(2)}) collective-permute-start(f32[16,512]{1,0:T(8,128)S(1)} %shard_map.64), channel_id=1, source_target_pairs={{0,8},{1,9},{2,10},{3,11},{4,12},{5,13},{6,14},{7,15},{8,0},{9,1},... | collective-permute-start | bytes 98312 | tf_op jit(solution)/shard_map/ppermute | solution.py:150
  5.1 0.0 collective-permute-done
  5.1 0.0 copy-start
  5.1 2.6 %collective-permute-start.2 = (f32[32,512]{1,0:T(8,128)S(1)}, f32[32,512]{1,0:T(8,128)S(1)}, u32[]{:S(2)}, u32[]{:S(2)}) collective-permute-start(f32[32,512]{1,0:T(8,128)S(1)} %pad_maximum_fusion.2.refs_3_), channel_id=1, source_target_pairs={{0,6},{1,15},{2,4},{3,13},{4,2},{5,11},{6,0},{7,9},{8,14},{9,7},{1... | collective-permute-start | bytes 196616 | tf_op jit(solution)/shard_map/ppermute | solution.py:150
  7.7 0.4 %collective-permute-start.1 = (f32[32,512]{1,0:T(8,128)S(1)}, f32[32,512]{1,0:T(8,128)S(1)}, u32[]{:S(2)}, u32[]{:S(2)}) collective-permute-start(f32[32,512]{1,0:T(8,128)S(1)} %pad_maximum_fusion.2.refs_3_), channel_id=1, source_target_pairs={{0,4},{1,11},{2,6},{3,9},{4,0},{5,15},{6,2},{7,13},{8,12},{9,3},{1... | collective-permute-start | bytes 196616 | tf_op jit(solution)/shard_map/ppermute | solution.py:150
  8.1 0.1 pad_add_fusion.owner
  8.2 0.5 %collective-permute-start.4 = (f32[32,512]{1,0:T(8,128)S(1)}, f32[32,512]{1,0:T(8,128)S(1)}, u32[]{:S(2)}, u32[]{:S(2)}) collective-permute-start(f32[32,512]{1,0:T(8,128)S(1)} %pad_maximum_fusion.2.refs_3_), channel_id=1, source_target_pairs={{0,2},{1,13},{2,0},{3,15},{4,6},{5,9},{6,4},{7,11},{8,10},{9,5},{1... | collective-permute-start | bytes 196616 | tf_op jit(solution)/shard_map/ppermute | solution.py:150
  8.7 0.0 copy-done
  8.7 0.0 copy-done.1
  8.7 0.1 copy-done.3
  8.8 0.0 copy-done.2
  8.8 1.1 %shard_map.65 = (bf16[256,256]{1,0:T(8,128)(2,1)S(1)}, bf16[256,256]{1,0:T(8,128)(2,1)S(1)}) custom-call(s32[2]{0:T(128)S(1)} %pad_add_fusion.owner, f32[16,16]{1,0:T(8,128)S(1)} %copy-done, f32[16,16]{1,0:T(8,128)S(1)} %copy-done.1, s32[4,4]{1,0:T(4,128)S(1)} %copy-done.2, s32[4,4]{1,0:T(4,128)S(1)} %copy-done.3), custom_call_target="tpu_custom_call" | custom-call | tf_op jit(solution)/shard_map/pallas_call | solution.py:181
  9.9 0.5 %collective-permute-done.2.refs_7_ = f32[32,512]{1,0:T(8,128)S(1)} collective-permute-done((f32[32,512]{1,0:T(8,128)S(1)}, f32[32,512]{1,0:T(8,128)S(1)}, u32[]{:S(2)}, u32[]{:S(2)}) %collective-permute-start.2) | collective-permute-done | bytes 65568 | tf_op jit(solution)/shard_map/ppermute | solution.py:150
  10.3 2.4 %collective-permute-done.1.refs_6_ = f32[32,512]{1,0:T(8,128)S(1)} collective-permute-done((f32[32,512]{1,0:T(8,128)S(1)}, f32[32,512]{1,0:T(8,128)S(1)}, u32[]{:S(2)}, u32[]{:S(2)}) %collective-permute-start.1) | collective-permute-done | bytes 65568 | tf_op jit(solution)/shard_map/ppermute | solution.py:150
  12.8 0.5 %collective-permute-start.6 = (f32[64,512]{1,0:T(8,128)S(1)}, f32[64,512]{1,0:T(8,128)S(1)}, u32[]{:S(2)}, u32[]{:S(2)}) collective-permute-start(f32[64,512]{1,0:T(8,128)S(1)} %pad_maximum_fusion), channel_id=1, source_target_pairs={{0,1},{1,0},{2,3},{3,2},{4,5},{5,4},{6,7},{7,6},{8,9},{9,8},{10,11... | collective-permute-start | bytes 393224 | tf_op jit(solution)/shard_map/ppermute | solution.py:150
  13.3 0.0 collective-permute-done.3.refs_4_
  13.3 0.0 collective-permute-done.4.refs_5_
  13.3 0.6 %collective-permute-start.5 = (f32[48,512]{1,0:T(8,128)S(1)}, f32[48,512]{1,0:T(8,128)S(1)}, u32[]{:S(2)}, u32[]{:S(2)}) collective-permute-start(f32[48,512]{1,0:T(8,128)S(1)} %pad_maximum_fusion.1), channel_id=1, source_target_pairs={{0,1},{1,0},{2,3},{3,2},{4,5},{5,4},{6,7},{7,6},{8,9},{9,8},{10,11... | collective-permute-start | bytes 294920 | tf_op jit(solution)/shard_map/ppermute | solution.py:150
  13.8 0.9 %collective-permute-done.5.refs_8_ = f32[48,512]{1,0:T(8,128)S(1)} collective-permute-done((f32[48,512]{1,0:T(8,128)S(1)}, f32[48,512]{1,0:T(8,128)S(1)}, u32[]{:S(2)}, u32[]{:S(2)}) %collective-permute-start.5) | collective-permute-done | bytes 98336 | tf_op jit(solution)/shard_map/ppermute | solution.py:150
  14.8 0.0 collective-permute-done.6.refs_9_
  14.8 1.2 %shard_map.66 = f32[128,512]{1,0:T(8,128)} custom-call(s32[1]{0:T(128)} %bitcast.refs_0_, bf16[256,256]{1,0:T(8,128)(2,1)S(1)} %get-tuple-element.14.refs_1_, bf16[256,256]{1,0:T(8,128)(2,1)S(1)} %get-tuple-element.15.refs_2_, f32[32,512]{1,0:T(8,128)S(1)} %pad_maximum_fusion.2.refs_3_, f32[16,512]{1,0:T(8,128)S(1)} %collective-permute-done.3.refs_4_, ...), custom_call_target="tpu_custom_call" | custom-call | tf_op jit(solution)/shard_map/pallas_call | solution.py:192
  (7 shorter events, 0.0 us)
Async XLA Ops:
  1.0 4.1 %collective-permute-start = (f32[16,512]{1,0:T(8,128)S(1)}, f32[16,512]{1,0:T(8,128)S(1)}, u32[]{:S(2)}, u32[]{:S(2)}) collective-permute-start(f32[16,512]{1,0:T(8,128)S(1)} %shard_map.64), channel_id=1, source_target_pairs={{0,1},{1,0},{2,3},{3,2},{4,5},{5,4},{6,7},{7,6},{8,9},{9,8},{10,11... | collective-permute-start | bytes 98312 | tf_op jit(solution)/shard_map/ppermute | solution.py:150
  1.4 11.8 %collective-permute-start.3 = (f32[16,512]{1,0:T(8,128)S(1)}, f32[16,512]{1,0:T(8,128)S(1)}, u32[]{:S(2)}, u32[]{:S(2)}) collective-permute-start(f32[16,512]{1,0:T(8,128)S(1)} %shard_map.64), channel_id=1, source_target_pairs={{0,8},{1,9},{2,10},{3,11},{4,12},{5,13},{6,14},{7,15},{8,0},{9,1},... | collective-permute-start | bytes 98312 | tf_op jit(solution)/shard_map/ppermute | solution.py:150
  5.1 3.7 %copy-start = (f32[16,16]{1,0:T(8,128)S(1)}, f32[16,16]{1,0:T(8,128)}, u32[]{:S(2)}) copy-start(f32[16,16]{1,0:T(8,128)} %occupied.1) | copy-start | bytes 3076
  5.1 3.7 %copy-start.1 = (f32[16,16]{1,0:T(8,128)S(1)}, f32[16,16]{1,0:T(8,128)}, u32[]{:S(2)}) copy-start(f32[16,16]{1,0:T(8,128)} %virtual.1) | copy-start | bytes 3076
  5.1 5.2 %collective-permute-start.2 = (f32[32,512]{1,0:T(8,128)S(1)}, f32[32,512]{1,0:T(8,128)S(1)}, u32[]{:S(2)}, u32[]{:S(2)}) collective-permute-start(f32[32,512]{1,0:T(8,128)S(1)} %pad_maximum_fusion.2.refs_3_), channel_id=1, source_target_pairs={{0,6},{1,15},{2,4},{3,13},{4,2},{5,11},{6,0},{7,9},{8,14},{9,7},{1... | collective-permute-start | bytes 196616 | tf_op jit(solution)/shard_map/ppermute | solution.py:150
  7.7 5.1 %collective-permute-start.1 = (f32[32,512]{1,0:T(8,128)S(1)}, f32[32,512]{1,0:T(8,128)S(1)}, u32[]{:S(2)}, u32[]{:S(2)}) collective-permute-start(f32[32,512]{1,0:T(8,128)S(1)} %pad_maximum_fusion.2.refs_3_), channel_id=1, source_target_pairs={{0,4},{1,11},{2,6},{3,9},{4,0},{5,15},{6,2},{7,13},{8,12},{9,3},{1... | collective-permute-start | bytes 196616 | tf_op jit(solution)/shard_map/ppermute | solution.py:150
  8.1 0.7 %copy-start.3 = (s32[4,4]{1,0:T(4,128)S(1)}, s32[4,4]{1,0:T(4,128)}, u32[]{:S(2)}) copy-start(s32[4,4]{1,0:T(4,128)} %virt_mask.1) | copy-start | bytes 196
  8.1 0.7 %copy-start.2 = (s32[4,4]{1,0:T(4,128)S(1)}, s32[4,4]{1,0:T(4,128)}, u32[]{:S(2)}) copy-start(s32[4,4]{1,0:T(4,128)} %occ_mask.1) | copy-start | bytes 196
  8.2 5.1 %collective-permute-start.4 = (f32[32,512]{1,0:T(8,128)S(1)}, f32[32,512]{1,0:T(8,128)S(1)}, u32[]{:S(2)}, u32[]{:S(2)}) collective-permute-start(f32[32,512]{1,0:T(8,128)S(1)} %pad_maximum_fusion.2.refs_3_), channel_id=1, source_target_pairs={{0,2},{1,13},{2,0},{3,15},{4,6},{5,9},{6,4},{7,11},{8,10},{9,5},{1... | collective-permute-start | bytes 196616 | tf_op jit(solution)/shard_map/ppermute | solution.py:150
  12.8 2.0 %collective-permute-start.6 = (f32[64,512]{1,0:T(8,128)S(1)}, f32[64,512]{1,0:T(8,128)S(1)}, u32[]{:S(2)}, u32[]{:S(2)}) collective-permute-start(f32[64,512]{1,0:T(8,128)S(1)} %pad_maximum_fusion), channel_id=1, source_target_pairs={{0,1},{1,0},{2,3},{3,2},{4,5},{5,4},{6,7},{7,6},{8,9},{9,8},{10,11... | collective-permute-start | bytes 393224 | tf_op jit(solution)/shard_map/ppermute | solution.py:150
  13.3 1.5 %collective-permute-start.5 = (f32[48,512]{1,0:T(8,128)S(1)}, f32[48,512]{1,0:T(8,128)S(1)}, u32[]{:S(2)}, u32[]{:S(2)}) collective-permute-start(f32[48,512]{1,0:T(8,128)S(1)} %pad_maximum_fusion.1), channel_id=1, source_target_pairs={{0,1},{1,0},{2,3},{3,2},{4,5},{5,4},{6,7},{7,6},{8,9},{9,8},{10,11... | collective-permute-start | bytes 294920 | tf_op jit(solution)/shard_map/ppermute | solution.py:150

commit v5 on v4

--- a/solution.py
+++ b/solution.py
@@ -184,6 +184,7 @@
         in_specs=[SMEM] + [VMEM] * 4,
         out_specs=(VMEM, VMEM),
         compiler_params=SMALL,
+        cost_estimate=pl.CostEstimate(flops=4 * basis * pairs * basis, bytes_accessed=4 * pairs * pairs, transcendentals=0),
     )(owner, occupied, virtual, occ_mask, virt_mask)
     cut = len(got) // 2
     early = exchange(jnp.concatenate(got[:cut], 0), 1, 1)
@@ -195,6 +196,7 @@
         in_specs=[SMEM] + [VMEM] * (2 + len(blocks)),
         out_specs=VMEM,
         compiler_params=SMALL,
+        cost_estimate=pl.CostEstimate(flops=6 * (aux // rows) * pairs * (pairs + aux), bytes_accessed=4 * pairs * (pairs + aux), transcendentals=0),
     )(lax.axis_index("row").reshape(1), high, low, *blocks)
 
 

time: 16.2 us -> 16.2 us (level)
  no operation moved by 1% of the time
where the time goes in v5:
time: 16.2 us; the launch traced here: 16 us
  starting transfers between devices  8.68 us (54%)
  waiting for transfers between devices  3.86 us (24%)
  Pallas kernels  2.4 us (15%)
  other arithmetic  0.96 us (6%)
    ppermute x7, starting transfers between devices, exchange(): lax.ppermute(block, axes, [(i, i ^ (odd if i % 2 else even)) for i in ran...  8.68 us
    ppermute x7, waiting for transfers between devices, exchange(): lax.ppermute(block, axes, [(i, i ^ (odd if i % 2 else even)) for i in ran...  3.86 us
    pallas_call x1, Pallas kernels, by_gathering(): pl.pallas_call(functools.partial(product_kernel, len(blocks)), out_shape=...  1.22 us
    pallas_call x1, Pallas kernels, by_gathering(): pl.pallas_call(functools.partial(mixing_kernel, order), out_shape=(mix, m...  1.05 us
    select_n x1, other arithmetic, by_gathering(): jnp.where(lax.broadcasted_iota(jnp.int32, wide_rows.shape, 0) < int_mask....  0.85 us
  transfers between devices with their start and end apart: 7, of which 3 were waited for; matrix products, arithmetic and copies ran while one was open for 1% of the time, Pallas kernels for 7%

profile of v5, /device:TPU:0, one launch (start us, length us, event | category | flops | bytes accessed | tf_op | source)
XLA Modules:
  0.0 16.0 jit_solution(16192941885356081273)
XLA Ops:
  0.0 0.9 %broadcast_select_fusion.packed = f32[20,1,512]{2,1,0:T(1,128)S(1)} fusion(pred[20]{0:T(512)(128)(4,1)S(1)} %iota_compare_fusion, f32[16,1,512]{2,1,0:T(1,128)} %param.6, s32[4,1,8]{2,1,0:T(1,128)} %param.9), kind=kLoop, calls=%fused_computation.2 | loop fusion | flops 20480 | bytes 73876 | tf_op jit(solution)/shard_map/jit(_where)/select_n | solution.py:158
  0.9 0.1 shard_map.64
  1.0 0.5 %collective-permute-start = (f32[16,512]{1,0:T(8,128)S(1)}, f32[16,512]{1,0:T(8,128)S(1)}, u32[]{:S(2)}, u32[]{:S(2)}) collective-permute-start(f32[16,512]{1,0:T(8,128)S(1)} %shard_map.64), channel_id=1, source_target_pairs={{0,1},{1,0},{2,3},{3,2},{4,5},{5,4},{6,7},{7,6},{8,9},{9,8},{10,11... | collective-permute-start | bytes 98312 | tf_op jit(solution)/shard_map/ppermute | solution.py:150
  1.4 3.6 %collective-permute-start.3 = (f32[16,512]{1,0:T(8,128)S(1)}, f32[16,512]{1,0:T(8,128)S(1)}, u32[]{:S(2)}, u32[]{:S(2)}) collective-permute-start(f32[16,512]{1,0:T(8,128)S(1)} %shard_map.64), channel_id=1, source_target_pairs={{0,8},{1,9},{2,10},{3,11},{4,12},{5,13},{6,14},{7,15},{8,0},{9,1},... | collective-permute-start | bytes 98312 | tf_op jit(solution)/shard_map/ppermute | solution.py:150
  5.1 0.0 collective-permute-done
  5.1 0.0 copy-start
  5.1 2.6 %collective-permute-start.2 = (f32[32,512]{1,0:T(8,128)S(1)}, f32[32,512]{1,0:T(8,128)S(1)}, u32[]{:S(2)}, u32[]{:S(2)}) collective-permute-start(f32[32,512]{1,0:T(8,128)S(1)} %pad_maximum_fusion.2.refs_3_), channel_id=1, source_target_pairs={{0,6},{1,15},{2,4},{3,13},{4,2},{5,11},{6,0},{7,9},{8,14},{9,7},{1... | collective-permute-start | bytes 196616 | tf_op jit(solution)/shard_map/ppermute | solution.py:150
  7.7 0.4 %collective-permute-start.1 = (f32[32,512]{1,0:T(8,128)S(1)}, f32[32,512]{1,0:T(8,128)S(1)}, u32[]{:S(2)}, u32[]{:S(2)}) collective-permute-start(f32[32,512]{1,0:T(8,128)S(1)} %pad_maximum_fusion.2.refs_3_), channel_id=1, source_target_pairs={{0,4},{1,11},{2,6},{3,9},{4,0},{5,15},{6,2},{7,13},{8,12},{9,3},{1... | collective-permute-start | bytes 196616 | tf_op jit(solution)/shard_map/ppermute | solution.py:150
  8.1 0.1 pad_add_fusion.owner
  8.2 0.5 %collective-permute-start.4 = (f32[32,512]{1,0:T(8,128)S(1)}, f32[32,512]{1,0:T(8,128)S(1)}, u32[]{:S(2)}, u32[]{:S(2)}) collective-permute-start(f32[32,512]{1,0:T(8,128)S(1)} %pad_maximum_fusion.2.refs_3_), channel_id=1, source_target_pairs={{0,2},{1,13},{2,0},{3,15},{4,6},{5,9},{6,4},{7,11},{8,10},{9,5},{1... | collective-permute-start | bytes 196616 | tf_op jit(solution)/shard_map/ppermute | solution.py:150
  8.7 0.0 copy-done
  8.7 0.0 copy-done.1
  8.7 0.1 copy-done.3
  8.8 0.0 copy-done.2
  8.8 1.1 %shard_map.65 = (bf16[256,256]{1,0:T(8,128)(2,1)S(1)}, bf16[256,256]{1,0:T(8,128)(2,1)S(1)}) custom-call(s32[2]{0:T(128)S(1)} %pad_add_fusion.owner, f32[16,16]{1,0:T(8,128)S(1)} %copy-done, f32[16,16]{1,0:T(8,128)S(1)} %copy-done.1, s32[4,4]{1,0:T(4,128)S(1)} %copy-done.2, s32[4,4]{1,0:T(4,128)S(1)} %copy-done.3), custom_call_target="tpu_custom_call" | custom-call | flops 262144 | bytes 262144 | tf_op jit(solution)/shard_map/pallas_call | solution.py:181
  9.9 0.5 %collective-permute-done.2.refs_7_ = f32[32,512]{1,0:T(8,128)S(1)} collective-permute-done((f32[32,512]{1,0:T(8,128)S(1)}, f32[32,512]{1,0:T(8,128)S(1)}, u32[]{:S(2)}, u32[]{:S(2)}) %collective-permute-start.2) | collective-permute-done | bytes 65568 | tf_op jit(solution)/shard_map/ppermute | solution.py:150
  10.3 2.4 %collective-permute-done.1.refs_6_ = f32[32,512]{1,0:T(8,128)S(1)} collective-permute-done((f32[32,512]{1,0:T(8,128)S(1)}, f32[32,512]{1,0:T(8,128)S(1)}, u32[]{:S(2)}, u32[]{:S(2)}) %collective-permute-start.1) | collective-permute-done | bytes 65568 | tf_op jit(solution)/shard_map/ppermute | solution.py:150
  12.8 0.5 %collective-permute-start.6 = (f32[64,512]{1,0:T(8,128)S(1)}, f32[64,512]{1,0:T(8,128)S(1)}, u32[]{:S(2)}, u32[]{:S(2)}) collective-permute-start(f32[64,512]{1,0:T(8,128)S(1)} %pad_maximum_fusion), channel_id=1, source_target_pairs={{0,1},{1,0},{2,3},{3,2},{4,5},{5,4},{6,7},{7,6},{8,9},{9,8},{10,11... | collective-permute-start | bytes 393224 | tf_op jit(solution)/shard_map/ppermute | solution.py:150
  13.3 0.0 collective-permute-done.3.refs_4_
  13.3 0.0 collective-permute-done.4.refs_5_
  13.3 0.6 %collective-permute-start.5 = (f32[48,512]{1,0:T(8,128)S(1)}, f32[48,512]{1,0:T(8,128)S(1)}, u32[]{:S(2)}, u32[]{:S(2)}) collective-permute-start(f32[48,512]{1,0:T(8,128)S(1)} %pad_maximum_fusion.1), channel_id=1, source_target_pairs={{0,1},{1,0},{2,3},{3,2},{4,5},{5,4},{6,7},{7,6},{8,9},{9,8},{10,11... | collective-permute-start | bytes 294920 | tf_op jit(solution)/shard_map/ppermute | solution.py:150
  13.8 0.9 %collective-permute-done.5.refs_8_ = f32[48,512]{1,0:T(8,128)S(1)} collective-permute-done((f32[48,512]{1,0:T(8,128)S(1)}, f32[48,512]{1,0:T(8,128)S(1)}, u32[]{:S(2)}, u32[]{:S(2)}) %collective-permute-start.5) | collective-permute-done | bytes 98336 | tf_op jit(solution)/shard_map/ppermute | solution.py:150
  14.8 0.0 collective-permute-done.6.refs_9_
  14.8 1.2 %shard_map.66 = f32[128,512]{1,0:T(8,128)} custom-call(s32[1]{0:T(128)} %bitcast.refs_0_, bf16[256,256]{1,0:T(8,128)(2,1)S(1)} %get-tuple-element.14.refs_1_, bf16[256,256]{1,0:T(8,128)(2,1)S(1)} %get-tuple-element.15.refs_2_, f32[32,512]{1,0:T(8,128)S(1)} %pad_maximum_fusion.2.refs_3_, f32[16,512]{1,0:T(8,128)S(1)} %collective-permute-done.3.refs_4_, ...), custom_call_target="tpu_custom_call" | custom-call | flops 150994944 | bytes 786432 | tf_op jit(solution)/shard_map/pallas_call | solution.py:193
  (7 shorter events, 0.0 us)
Async XLA Ops:
  1.0 4.1 %collective-permute-start = (f32[16,512]{1,0:T(8,128)S(1)}, f32[16,512]{1,0:T(8,128)S(1)}, u32[]{:S(2)}, u32[]{:S(2)}) collective-permute-start(f32[16,512]{1,0:T(8,128)S(1)} %shard_map.64), channel_id=1, source_target_pairs={{0,1},{1,0},{2,3},{3,2},{4,5},{5,4},{6,7},{7,6},{8,9},{9,8},{10,11... | collective-permute-start | bytes 98312 | tf_op jit(solution)/shard_map/ppermute | solution.py:150
  1.4 11.8 %collective-permute-start.3 = (f32[16,512]{1,0:T(8,128)S(1)}, f32[16,512]{1,0:T(8,128)S(1)}, u32[]{:S(2)}, u32[]{:S(2)}) collective-permute-start(f32[16,512]{1,0:T(8,128)S(1)} %shard_map.64), channel_id=1, source_target_pairs={{0,8},{1,9},{2,10},{3,11},{4,12},{5,13},{6,14},{7,15},{8,0},{9,1},... | collective-permute-start | bytes 98312 | tf_op jit(solution)/shard_map/ppermute | solution.py:150
  5.1 3.7 %copy-start = (f32[16,16]{1,0:T(8,128)S(1)}, f32[16,16]{1,0:T(8,128)}, u32[]{:S(2)}) copy-start(f32[16,16]{1,0:T(8,128)} %occupied.1) | copy-start | bytes 3076
  5.1 3.7 %copy-start.1 = (f32[16,16]{1,0:T(8,128)S(1)}, f32[16,16]{1,0:T(8,128)}, u32[]{:S(2)}) copy-start(f32[16,16]{1,0:T(8,128)} %virtual.1) | copy-start | bytes 3076
  5.1 5.2 %collective-permute-start.2 = (f32[32,512]{1,0:T(8,128)S(1)}, f32[32,512]{1,0:T(8,128)S(1)}, u32[]{:S(2)}, u32[]{:S(2)}) collective-permute-start(f32[32,512]{1,0:T(8,128)S(1)} %pad_maximum_fusion.2.refs_3_), channel_id=1, source_target_pairs={{0,6},{1,15},{2,4},{3,13},{4,2},{5,11},{6,0},{7,9},{8,14},{9,7},{1... | collective-permute-start | bytes 196616 | tf_op jit(solution)/shard_map/ppermute | solution.py:150
  7.7 5.1 %collective-permute-start.1 = (f32[32,512]{1,0:T(8,128)S(1)}, f32[32,512]{1,0:T(8,128)S(1)}, u32[]{:S(2)}, u32[]{:S(2)}) collective-permute-start(f32[32,512]{1,0:T(8,128)S(1)} %pad_maximum_fusion.2.refs_3_), channel_id=1, source_target_pairs={{0,4},{1,11},{2,6},{3,9},{4,0},{5,15},{6,2},{7,13},{8,12},{9,3},{1... | collective-permute-start | bytes 196616 | tf_op jit(solution)/shard_map/ppermute | solution.py:150
  8.1 0.7 %copy-start.3 = (s32[4,4]{1,0:T(4,128)S(1)}, s32[4,4]{1,0:T(4,128)}, u32[]{:S(2)}) copy-start(s32[4,4]{1,0:T(4,128)} %virt_mask.1) | copy-start | bytes 196
  8.1 0.7 %copy-start.2 = (s32[4,4]{1,0:T(4,128)S(1)}, s32[4,4]{1,0:T(4,128)}, u32[]{:S(2)}) copy-start(s32[4,4]{1,0:T(4,128)} %occ_mask.1) | copy-start | bytes 196
  8.2 5.1 %collective-permute-start.4 = (f32[32,512]{1,0:T(8,128)S(1)}, f32[32,512]{1,0:T(8,128)S(1)}, u32[]{:S(2)}, u32[]{:S(2)}) collective-permute-start(f32[32,512]{1,0:T(8,128)S(1)} %pad_maximum_fusion.2.refs_3_), channel_id=1, source_target_pairs={{0,2},{1,13},{2,0},{3,15},{4,6},{5,9},{6,4},{7,11},{8,10},{9,5},{1... | collective-permute-start | bytes 196616 | tf_op jit(solution)/shard_map/ppermute | solution.py:150
  12.8 2.0 %collective-permute-start.6 = (f32[64,512]{1,0:T(8,128)S(1)}, f32[64,512]{1,0:T(8,128)S(1)}, u32[]{:S(2)}, u32[]{:S(2)}) collective-permute-start(f32[64,512]{1,0:T(8,128)S(1)} %pad_maximum_fusion), channel_id=1, source_target_pairs={{0,1},{1,0},{2,3},{3,2},{4,5},{5,4},{6,7},{7,6},{8,9},{9,8},{10,11... | collective-permute-start | bytes 393224 | tf_op jit(solution)/shard_map/ppermute | solution.py:150
  13.3 1.5 %collective-permute-start.5 = (f32[48,512]{1,0:T(8,128)S(1)}, f32[48,512]{1,0:T(8,128)S(1)}, u32[]{:S(2)}, u32[]{:S(2)}) collective-permute-start(f32[48,512]{1,0:T(8,128)S(1)} %pad_maximum_fusion.1), channel_id=1, source_target_pairs={{0,1},{1,0},{2,3},{3,2},{4,5},{5,4},{6,7},{7,6},{8,9},{9,8},{10,11... | collective-permute-start | bytes 294920 | tf_op jit(solution)/shard_map/ppermute | solution.py:150
